TPU v7x, 128 devices: a whole 4x4x4 slice. The times are simulated.
128 devices in a mesh: group: 4 (over z_hi, core), tensor: 32 (over z_lo, y, x).
Axes of the slice: x: 4, y: 4, z: 4 (z_hi: 2, z_lo: 2; z = z_hi * 2 + z_lo), core: 2. Of those that a mesh axis runs over, the one named last changes fastest.
Arguments:
- hidden: bfloat16 [1024, 2, 8192], P('group', None, 'tensor'), may hold values from -6 to 6
- query_weight: bfloat16 [8192, 8192], P(None, 'tensor'), may hold values from -0.0625 to 0.0625
- key_weight: bfloat16 [8192, 1024], P(None, 'tensor'), may hold values from -0.0625 to 0.0625
- value_weight: bfloat16 [8192, 1024], P(None, 'tensor'), may hold values from -0.0625 to 0.0625
- output_weight: bfloat16 [8192, 8192], P('tensor'), may hold values from -0.25 to 0.25
- adapter_down_maps: bfloat16 [32, 8192, 128], P(None, 'tensor'), may hold values from -0.0625 to 0.0625
- adapter_up_query: bfloat16 [32, 64, 8192], P(None, None, 'tensor'), may hold values from -0.75 to 0.75
- adapter_up_value: bfloat16 [32, 64, 1024], P(None, None, 'tensor'), may hold values from -0.75 to 0.75
- key_value_pages: bfloat16 [4096, 64, 2048], P(('group', 'tensor')), may hold values from -1300 to 1300
- row_adapter_index: int32 [1024], P('group'), may hold values from 0 to 31
- row_rank_bucket: int32 [1024], P('group'), may hold values from 16 to 64, as said below
- lengths: int32 [1024], replicated, may hold values from 1 to 256, as said below
- row_page_index: int32 [1024, 4], replicated, may hold values from 0 to 4095, as said below
Outputs:
- output: bfloat16 [1024, 2, 8192], P('group', None, 'tensor')
Inputs may be any that keep to these rules, and one draw needn't show every extreme that they name: `row_page_index`: every page id is used by exactly one (row, slot). Device d = r // 8 numbers the devices group after group. A row is either local, with all its pages in the ids d * 8 * 4 to (d + 1) * 8 * 4 - 1 of its own device, or resumed, with all of them in the ids of the device with the same tensor index in the next group, cyclically. The rows of each device, 8 in an aligned block, hold exactly 4 resumed rows. `lengths`: the rows of each device include one of length 256. `row_rank_bucket`: one of 64, 32 and 16.
All inputs are finite; a program needn't handle non-finite values.
Results may differ from a plain program's by a relative error of at most 0.03.
Values may be sent and summed in bfloat16 or wider, within the bound.
A program may use at most 192 MiB of HBM per device.

v0:
```python
import math

import jax
import jax.numpy as jnp
from jax import lax
from jax.sharding import PartitionSpec as P

QUERY_HEADS = 64
KEY_VALUE_HEADS = 8
HEAD_SIZE = 128
RANK_LIMIT = 64
STEPS = 2
RES = 4


ROPE_BASE = 500000.0


def from_behind(block, axis, distance):
    devices = range(lax.axis_size(axis))
    route = [((i - distance) % len(devices), i) for i in devices]
    return lax.ppermute(block, axis, route)


def rotate(values, positions):
    half_dim = values.shape[-1] // 2
    inverse_freq = jnp.exp(
        -math.log(ROPE_BASE) * jnp.arange(half_dim, dtype=jnp.float32) / half_dim
    )
    angles = positions.astype(jnp.float32)[..., None, None] * inverse_freq
    cos_part = jnp.cos(angles)
    sin_part = jnp.sin(angles)
    first_half = values[..., :half_dim]
    second_half = values[..., half_dim:]
    return jnp.concatenate(
        [
            first_half * cos_part - second_half * sin_part,
            second_half * cos_part + first_half * sin_part,
        ],
        axis=-1,
    )


def attend(query_rows, kv_cache, keys_new, fresh_value_rows, row_lengths):
    batch_rows = kv_cache.shape[0]
    ctx_len = kv_cache.shape[1]
    key_block = jnp.concatenate(
        [kv_cache[:, :, : KEY_VALUE_HEADS * HEAD_SIZE], keys_new], axis=1
    ).reshape(batch_rows, ctx_len + STEPS, KEY_VALUE_HEADS, HEAD_SIZE)
    value_block = jnp.concatenate(
        [kv_cache[:, :, KEY_VALUE_HEADS * HEAD_SIZE :], fresh_value_rows], axis=1
    ).reshape(batch_rows, ctx_len + STEPS, KEY_VALUE_HEADS, HEAD_SIZE)
    grouped = query_rows.reshape(
        batch_rows, STEPS, KEY_VALUE_HEADS, QUERY_HEADS // KEY_VALUE_HEADS, HEAD_SIZE
    )
    scores = jnp.einsum(
        "rsngd,rtnd->rsngt", grouped, key_block, preferred_element_type=jnp.float32
    ) * HEAD_SIZE ** (-0.5)
    slot_pos = jnp.arange(ctx_len + STEPS)
    step_pos = jnp.arange(STEPS)
    in_cache = slot_pos[None, None, :] < row_lengths[:, None, None]
    in_steps = slot_pos[None, :] - ctx_len <= step_pos[:, None]
    usable = jnp.where(slot_pos[None, None, :] < ctx_len, in_cache, in_steps[None, :, :])[
        :, :, None, None, :
    ]
    peak_score = jnp.max(jnp.where(usable, scores, -jnp.inf), axis=-1, keepdims=True)
    weights_raw = jnp.where(usable, jnp.exp(scores - peak_score), 0.0)
    totals = jnp.sum(weights_raw, axis=-1)
    mixture = jnp.einsum(
        "rsngt,rtnd->rsngd",
        weights_raw.astype(jnp.bfloat16),
        value_block,
        preferred_element_type=jnp.float32,
    )
    return (
        (mixture / totals[..., None])
        .astype(jnp.bfloat16)
        .reshape(batch_rows, STEPS, QUERY_HEADS * HEAD_SIZE)
    )


def pick_resumed(flags):
    order_pos = jnp.cumsum(flags) - flags
    match = (flags[None, :] == 1) & (order_pos[None, :] == jnp.arange(RES)[:, None])
    return jnp.sum(jnp.where(match, jnp.arange(flags.shape[0])[None, :], 0), axis=1)


def local(
    hidden,
    query_weight,
    key_weight,
    value_weight,
    output_weight,
    adapter_down_maps,
    adapter_up_query,
    adapter_up_value,
    key_value_pages,
    row_adapter_index,
    row_rank_bucket,
    lengths,
    row_page_index,
):
    group_rows = hidden.shape[0]
    step_count = hidden.shape[1]
    tensors = lax.axis_size("tensor")
    groups = lax.axis_size("group")
    group_index = lax.axis_index("group")
    tensor_index = lax.axis_index("tensor")
    rows_dev = group_rows // tensors
    pool_size = key_value_pages.shape[0]
    channels = key_value_pages.shape[2]
    row_down_maps = adapter_down_maps[row_adapter_index]
    local_low = jnp.einsum(
        "rsd,rdk->rsk", hidden, row_down_maps, preferred_element_type=jnp.float32
    ).astype(jnp.bfloat16)
    gathered, low_parts = (
        lax.all_gather(hidden, "tensor", axis=2, tiled=True),
        lax.all_gather(local_low, "tensor", axis=2, tiled=True),
    )
    lowrank = jnp.sum(
        low_parts.reshape(group_rows, step_count, tensors, 2 * RANK_LIMIT).astype(jnp.float32),
        axis=2,
    )
    column = jnp.arange(2 * RANK_LIMIT) % RANK_LIMIT
    bucket = row_rank_bucket[:, None, None]
    scaled = jnp.where(
        column[None, None, :] < bucket,
        lowrank * (0.5 * RANK_LIMIT) / bucket.astype(jnp.float32),
        0.0,
    ).astype(jnp.bfloat16)
    row_query_up_maps = adapter_up_query[row_adapter_index]
    row_value_up_maps = adapter_up_value[row_adapter_index]
    lift_query = jnp.einsum(
        "rsk,rkn->rsn",
        scaled[:, :, :RANK_LIMIT],
        row_query_up_maps,
        preferred_element_type=jnp.float32,
    ).reshape(group_rows * step_count, -1)
    lift_value = jnp.einsum(
        "rsk,rkn->rsn",
        scaled[:, :, RANK_LIMIT:],
        row_value_up_maps,
        preferred_element_type=jnp.float32,
    ).reshape(group_rows * step_count, -1)
    flat_layout = gathered.reshape(group_rows * step_count, -1)
    query_rows = jnp.dot(flat_layout, query_weight, preferred_element_type=jnp.float32) + lift_query
    keys_new = jnp.dot(flat_layout, key_weight, preferred_element_type=jnp.float32)
    fresh_value_rows = (
        jnp.dot(flat_layout, value_weight, preferred_element_type=jnp.float32) + lift_value
    )
    query_rows = query_rows.astype(jnp.bfloat16).reshape(group_rows, step_count, -1)
    keys_new = keys_new.astype(jnp.bfloat16).reshape(group_rows, step_count, -1)
    fresh_value_rows = fresh_value_rows.astype(jnp.bfloat16).reshape(group_rows, step_count, -1)
    query_rows, keys_new, fresh_value_rows = (
        lax.all_to_all(query_rows, "tensor", split_axis=0, concat_axis=2, tiled=True),
        lax.all_to_all(keys_new, "tensor", split_axis=0, concat_axis=2, tiled=True),
        lax.all_to_all(fresh_value_rows, "tensor", split_axis=0, concat_axis=2, tiled=True),
    )
    first_row = group_index * group_rows + tensor_index * rows_dev
    my_lengths = lax.dynamic_slice_in_dim(lengths, first_row, rows_dev)
    positions = my_lengths[:, None] + jnp.arange(step_count, dtype=jnp.int32)[None, :]
    rotated_queries = (
        rotate(
            query_rows.astype(jnp.float32).reshape(rows_dev, step_count, QUERY_HEADS, HEAD_SIZE),
            positions,
        )
        .astype(jnp.bfloat16)
        .reshape(rows_dev, step_count, QUERY_HEADS * HEAD_SIZE)
    )
    rotated_keys = (
        rotate(
            keys_new.astype(jnp.float32).reshape(rows_dev, step_count, KEY_VALUE_HEADS, HEAD_SIZE),
            positions,
        )
        .astype(jnp.bfloat16)
        .reshape(rows_dev, step_count, KEY_VALUE_HEADS * HEAD_SIZE)
    )
    my_device = group_index * tensors + tensor_index
    my_base = my_device * pool_size
    my_table = lax.dynamic_slice_in_dim(row_page_index, first_row, rows_dev, 0)
    my_flags = (my_table[:, 0] // pool_size != my_device).astype(jnp.int32)
    own_ids = jnp.clip(my_table - my_base, 0, pool_size - 1)
    local_cache = key_value_pages[own_ids].reshape(rows_dev, -1, channels)
    slot_of = jnp.clip(jnp.cumsum(my_flags) - my_flags, 0, RES - 1)
    prior_group = (group_index + groups - 1) % groups
    prior_first = prior_group * group_rows + tensor_index * rows_dev
    prior_device = prior_group * tensors + tensor_index
    prior_table = lax.dynamic_slice_in_dim(row_page_index, prior_first, rows_dev, 0)
    prior_flags = (prior_table[:, 0] // pool_size != prior_device).astype(jnp.int32)
    picked = pick_resumed(prior_flags)
    lent_ids = jnp.clip(prior_table[picked] - my_base, 0, pool_size - 1)
    lent_pages = key_value_pages[lent_ids]
    borrowed = from_behind(lent_pages, "group", -1)
    fetched = borrowed.reshape(RES, -1, channels)[slot_of]
    kv_cache = jnp.where(my_flags[:, None, None] == 1, fetched, local_cache)
    attended = attend(rotated_queries, kv_cache, rotated_keys, fresh_value_rows, my_lengths)
    returned = lax.all_to_all(attended, "tensor", split_axis=2, concat_axis=0, tiled=True)
    partial_out = jnp.dot(
        returned.reshape(group_rows * step_count, -1),
        output_weight,
        preferred_element_type=jnp.float32,
    ).reshape(group_rows, step_count, -1)
    return lax.psum_scatter(
        partial_out.astype(jnp.bfloat16), "tensor", scatter_dimension=2, tiled=True
    )


def solution(mesh):
    in_specs = (
        P("group", None, "tensor"),
        P(None, "tensor"),
        P(None, "tensor"),
        P(None, "tensor"),
        P("tensor", None),
        P(None, "tensor", None),
        P(None, None, "tensor"),
        P(None, None, "tensor"),
        P(("group", "tensor"), None, None),
        P("group"),
        P("group"),
        P(),
        P(),
    )
    out_specs = P("group", None, "tensor")
    return jax.shard_map(local, mesh=mesh, in_specs=in_specs, out_specs=out_specs, check_vma=False)
```

profile of v0, /device:TPU:0, one launch (start us, length us, event | category | flops | bytes accessed | tf_op | source)
XLA Modules:
  0.0 674.8 jit_solution(3616432894510345260)
XLA Ops:
  8.1 9.6 %gather_fusion.4 = bf16[256,256,128]{2,1,0:T(8,128)(2,1)} fusion(bf16[32,256,128]{2,1,0:T(8,128)(2,1)S(1)} %copy-done, s32[1024]{0:T(1024)S(1)} %pad_clamp_fusion), kind=kCustom, calls=%fused_computation.4 | custom fusion | bytes 33555456 | tf_op jit(solution)/shard_map/gather | solution.py:112
  17.8 7.6 %fusion.16 = bf16[256,2,128]{2,1,0:T(2,128)(2,1)} fusion(bf16[256,256,128]{2,1,0:T(8,128)(2,1)} %gather_fusion.4, bf16[256,2,256]{2,1,0:T(2,128)(2,1)S(1)} %copy-done.6), kind=kOutput, calls=%fused_computation.31 | convolution fusion | flops 33619968 | bytes 17170432 | tf_op jit(solution)/shard_map/rsd,rdk->rsk/dot_general | solution.py:113
  28.2 6.2 gather_fusion.1
  38.0 8.5 %gather_fusion.3 = bf16[32,64,2048]{2,1,0:T(8,128)(2,1)} fusion(bf16[32,64,2048]{2,1,0:T(8,128)(2,1)} %param.21, s32[1024]{0:T(1024)S(1)} %pad_clamp_fusion.1), kind=kCustom, calls=%fused_computation.3 | custom fusion | bytes 16777344 | tf_op jit(solution)/shard_map/gather | solution.py:183
  47.2 8.6 %gather_fusion.6 = bf16[256,64,256]{2,1,0:T(8,128)(2,1)} fusion(bf16[32,64,256]{2,1,0:T(8,128)(2,1)S(1)} %copy-done.2, s32[1024]{0:T(1024)S(1)} %pad_clamp_fusion), kind=kCustom, calls=%fused_computation.6 | custom fusion | bytes 16778240 | tf_op jit(solution)/shard_map/gather | solution.py:131
  58.8 89.9 %collective-permute-done = bf16[4,4,64,2048]{3,2,1,0:T(8,128)(2,1)} collective-permute-done((bf16[4,4,64,2048]{3,2,1,0:T(8,128)(2,1)}, bf16[4,4,64,2048]{3,2,1,0:T(8,128)(2,1)}, u32[]{:S(2)}, u32[]{:S(2)}) %collective-permute-start) | collective-permute-done | bytes 4194336 | tf_op jit(solution)/shard_map/ppermute | solution.py:22
  148.7 6.9 %gather_fusion.2 = bf16[8,256,2048]{2,1,0:T(8,128)(2,1)} fusion(bf16[4,256,2048]{2,1,0:T(8,128)(2,1)} %bitcast.4, s32[1024]{0:T(1024)S(1)} %pad_clamp_fusion.2), kind=kCustom, calls=%fused_computation.2 | custom fusion | bytes 16777248 | tf_op jit(solution)/shard_map/gather | solution.py:194
  155.6 6.5 bitcast_select_fusion
  165.9 6.5 copy.87
  172.4 6.5 copy.92
  178.9 6.5 copy.81
  185.4 6.5 copy.85
  192.8 8.3 %reshape.335 = f32[256,2,32,128]{3,2,1,0:T(8,128)} reshape(bf16[256,2,4096]{2,1,0:T(2,128)(2,1)} %all-gather.5.cloned.1.call-done) | data formatting | bytes 12582912 | tf_op jit(solution)/shard_map/convert_element_type | solution.py:121
  213.0 155.8 %all-gather.3.cloned.1.call-done = bf16[256,2,8192]{2,1,0:T(2,128)(2,1)} async-done(((bf16[256,2,256]{2,1,0:T(2,128)(2,1)}), bf16[256,2,8192]{2,1,0:T(2,128)(2,1)}) %all-gather.3.cloned.1.call-update) | async-done | bytes 8388624 | tf_op jit(solution)/shard_map/all_gather | solution.py:117
  368.7 13.1 %reshape.328 = bf16[512,8192]{1,0:T(8,128)(2,1)} reshape(bf16[256,2,8192]{2,1,0:T(2,128)(2,1)} %all-gather.3.cloned.1.call-done) | data formatting | bytes 16777216 | tf_op jit(solution)/shard_map/reshape | solution.py:145
  388.8 6.9 %all-to-all-start.1 = ((bf16[32,2,256]{2,1,0:T(2,128)(2,1)}), bf16[32,2,256]{2,1,0:T(2,128)(2,1)S(1)}, u32[]{:S(2)}, u32[]{:S(2)}) async-start(bf16[32,2,256]{2,1,0:T(2,128)(2,1)} %reshape.412), calls=%async_computation.1 | async-start | bytes 65536 | tf_op jit(solution)/shard_map/all_to_all | solution.py:156
  404.0 6.9 %all-to-all-start = ((bf16[32,2,256]{2,1,0:T(2,128)(2,1)}), bf16[32,2,256]{2,1,0:T(2,128)(2,1)S(1)}, u32[]{:S(2)}, u32[]{:S(2)}) async-start(bf16[32,2,256]{2,1,0:T(2,128)(2,1)} %reshape.410), calls=%async_computation | async-start | bytes 65536 | tf_op jit(solution)/shard_map/all_to_all | solution.py:157
  411.0 6.9 %fusion.15 = bf16[512,256]{1,0:T(8,128)(2,1)S(1)} fusion(f32[512,256]{1,0:T(8,128)S(1)} %reshape.332, bf16[512,8192]{1,0:T(8,128)(2,1)} %reshape.328, bf16[8192,256]{1,0:T(8,128)(2,1)} %param.14), kind=kOutput, calls=%fused_computation.29 | convolution fusion | flops 2147745792 | bytes 13369344 | tf_op jit(solution)/shard_map/dot_general | solution.py:146
  419.3 8.0 %all-to-all-start.2 = ((bf16[256,2,256]{2,1,0:T(2,128)(2,1)}), bf16[256,2,256]{2,1,0:T(2,128)(2,1)S(1)}, u32[]{:S(2)}, u32[]{:S(2)}) async-start(bf16[256,2,256]{2,1,0:T(2,128)(2,1)} %reshape.333), calls=%async_computation.2 | async-start | bytes 524288 | tf_op jit(solution)/shard_map/all_to_all | solution.py:155
  427.9 8.4 %all-to-all-done.2 = bf16[256,2,256]{2,1,0:T(2,128)(2,1)S(1)} async-done(((bf16[256,2,256]{2,1,0:T(2,128)(2,1)}), bf16[256,2,256]{2,1,0:T(2,128)(2,1)S(1)}, u32[]{:S(2)}, u32[]{:S(2)}) %all-to-all-start.2) | async-done | bytes 262176 | tf_op jit(solution)/shard_map/all_to_all | solution.py:155
  452.8 12.8 %all_to_all.48 = bf16[32,2,2048]{2,1,0:T(2,128)(2,1)S(1)} all-to-all(bf16[32,2,2048]{2,1,0:T(2,128)(2,1)S(1)} %reshape.414), channel_id=1, replica_groups=mesh['group'=4,'tensor'=32] {'tensor'}, dimensions={0} | all-to-all | bytes 524288 | tf_op jit(solution)/shard_map/all_to_all | solution.py:197
  471.5 8.2 %copy.107 = bf16[8,2,32,256]{3,0,2,1:T(8,128)(2,1)S(1)} copy(bf16[8,2,32,256]{0,1,3,2:T(2,128)(2,1)} %bitcast.106) | data formatting | bytes 524288 | tf_op jit(solution)/shard_map/all_to_all | solution.py:197
  479.8 7.8 %convolution_convert_fusion = bf16[256,2,8192]{2,0,1:T(8,128)(2,1)} fusion(bf16[256,8192]{1,0:T(8,128)(2,1)} %param.17, bf16[8,2,32,256]{3,0,2,1:T(8,128)(2,1)S(1)} %copy.107), kind=kOutput, calls=%fused_computation.8 | convolution fusion | flops 2151677952 | bytes 12845056 | tf_op jit(solution)/shard_map/dot_general | solution.py:198
  487.6 178.8 %reduce-scatter.2.cloned.1.call-done = bf16[256,2,256]{2,0,1:T(8,128)(2,1)} async-done(((bf16[256,2,8192]{2,0,1:T(8,128)(2,1)}), bf16[256,2,256]{2,0,1:T(8,128)(2,1)}) %reduce-scatter.2.cloned.1.call-update) | async-done | bytes 262160 | tf_op jit(solution)/shard_map/reduce_scatter | solution.py:203
  (104 shorter events, 69.7 us)
Async XLA Ops:
  6.5 1.6 copy-start
  6.5 186.2 %all-gather.5.cloned.1.call-start = ((), (), s32[]{:S(2)}) async-start(), calls=%async_computation.6 | async-start | bytes 4325376 | tf_op jit(solution)/shard_map/all_gather | solution.py:118
  8.1 9.6 %copy-start.6 = (bf16[256,2,256]{2,1,0:T(2,128)(2,1)S(1)}, bf16[256,2,256]{2,1,0:T(2,128)(2,1)}, u32[]{:S(2)}) copy-start(bf16[256,2,256]{2,1,0:T(2,128)(2,1)} %param.13) | copy-start | bytes 786436
  25.4 343.3 %all-gather.3.cloned.1.call-start = ((), (), s32[]{:S(2)}) async-start(), calls=%async_computation.5 | async-start | bytes 8650752 | tf_op jit(solution)/shard_map/all_gather | solution.py:117
  34.3 114.4 %collective-permute-start = (bf16[4,4,64,2048]{3,2,1,0:T(8,128)(2,1)}, bf16[4,4,64,2048]{3,2,1,0:T(8,128)(2,1)}, u32[]{:S(2)}, u32[]{:S(2)}) collective-permute-start(bf16[4,4,64,2048]{3,2,1,0:T(8,128)(2,1)} %bitcast.107), channel_id=1, source_target_pairs={{32,0},{64,32},{96,64},{0,96},{33,1},{65,33},{97,65},{1,97},{34,2}... | collective-permute-start | bytes 12582920 | tf_op jit(solution)/shard_map/ppermute | solution.py:22
  38.0 9.3 %copy-start.9 = (s32[256]{0:T(256)S(1)}, s32[256]{0:T(256)}, u32[]{:S(2)}) copy-start(s32[256]{0:T(256)} %param.23) | copy-start | bytes 3076
  38.0 9.3 %copy-start.2 = (bf16[32,64,256]{2,1,0:T(8,128)(2,1)S(1)}, bf16[32,64,256]{2,1,0:T(8,128)(2,1)}, u32[]{:S(2)}) copy-start(bf16[32,64,256]{2,1,0:T(8,128)(2,1)} %param.19) | copy-start | bytes 3145732
  47.2 8.6 %copy-start.3 = (bf16[32,64,32]{1,2,0:T(8,128)(2,1)S(1)}, bf16[32,64,32]{1,2,0:T(8,128)(2,1)}, u32[]{:S(2)}) copy-start(bf16[32,64,32]{1,2,0:T(8,128)(2,1)} %param.20) | copy-start | bytes 393220
  206.4 5.2 copy-start.4
  213.0 168.9 %copy-start.7 = (bf16[8192,32]{0,1:T(8,128)(2,1)S(1)}, bf16[8192,32]{0,1:T(8,128)(2,1)}, u32[]{:S(2)}) copy-start(bf16[8192,32]{0,1:T(8,128)(2,1)} %param.15) | copy-start | bytes 1572868
  381.8 13.9 %copy-start.8 = (bf16[8192,32]{0,1:T(8,128)(2,1)S(1)}, bf16[8192,32]{0,1:T(8,128)(2,1)}, u32[]{:S(2)}) copy-start(bf16[8192,32]{0,1:T(8,128)(2,1)} %param.16) | copy-start | bytes 1572868
  388.8 15.3 %all-to-all-start.1 = ((bf16[32,2,256]{2,1,0:T(2,128)(2,1)}), bf16[32,2,256]{2,1,0:T(2,128)(2,1)S(1)}, u32[]{:S(2)}, u32[]{:S(2)}) async-start(bf16[32,2,256]{2,1,0:T(2,128)(2,1)} %reshape.412), calls=%async_computation.1 | async-start | bytes 65536 | tf_op jit(solution)/shard_map/all_to_all | solution.py:156
  404.0 15.2 %all-to-all-start = ((bf16[32,2,256]{2,1,0:T(2,128)(2,1)}), bf16[32,2,256]{2,1,0:T(2,128)(2,1)S(1)}, u32[]{:S(2)}, u32[]{:S(2)}) async-start(bf16[32,2,256]{2,1,0:T(2,128)(2,1)} %reshape.410), calls=%async_computation | async-start | bytes 65536 | tf_op jit(solution)/shard_map/all_to_all | solution.py:157
  419.3 17.0 %all-to-all-start.2 = ((bf16[256,2,256]{2,1,0:T(2,128)(2,1)}), bf16[256,2,256]{2,1,0:T(2,128)(2,1)S(1)}, u32[]{:S(2)}, u32[]{:S(2)}) async-start(bf16[256,2,256]{2,1,0:T(2,128)(2,1)} %reshape.333), calls=%async_computation.2 | async-start | bytes 524288 | tf_op jit(solution)/shard_map/all_to_all | solution.py:155
  427.3 239.0 %reduce-scatter.2.cloned.1.call-start = ((), (), s32[]{:S(2)}) async-start(), calls=%async_computation.7 | async-start | bytes 8650752 | tf_op jit(solution)/shard_map/reduce_scatter | solution.py:203
  436.7 4.5 copy-start.5
  487.5 180.7 %copy-start.1 = (bf16[32,256,128]{2,1,0:T(8,128)(2,1)S(1)}, bf16[32,256,128]{2,1,0:T(8,128)(2,1)}, u32[]{:S(2)}) copy-start(bf16[32,256,128]{2,1,0:T(8,128)(2,1)} %param.18) | copy-start | bytes 6291460
Sparse Core Ops, SparseCore 0:
  25.5 167.1 all-gather.4
  194.3 174.3 all-gather.2
  487.7 178.5 reduce-scatter.1
where the time goes:
time: 677 us; the launch traced here: 675 us
  waiting for transfers between devices  436 us (64%)
  local copies, waits for them, and re-layouts  127 us (19%)
  matrix products  44.9 us (7%)
  starting transfers between devices  25.4 us (4%)
  other arithmetic  14.8 us (2%)
  between operations  13.5 us (2%)
  blocking collectives  12.8 us (2%)
    reduce_scatter x1, waiting for transfers between devices, local(): lax.psum_scatter(partial_out.astype(jnp.bfloat16), 'tensor', scatter_dime...  179 us
    all_gather x1, waiting for transfers between devices, local(): lax.all_gather(hidden, 'tensor', axis=2, tiled=True)  156 us
    ppermute x1, waiting for transfers between devices, from_behind(): return lax.ppermute(block, axis, route)  89.9 us
    unnamed x28, local copies, waits for them, and re-layouts  14.5 us
  transfers between devices with their start and end apart: 7, of which 7 were waited for; matrix products, arithmetic and copies ran while one was open for 16% of the time, Pallas kernels for 0%

commit v1 on v0

v1 whole, which is shorter than its diff:
```python
import functools
import math

import jax
import jax.numpy as jnp
from jax import lax
from jax.experimental import pallas as pl
from jax.experimental.pallas import tpu as pltpu
from jax.sharding import PartitionSpec as P

QUERY_HEADS = 64
KEY_VALUE_HEADS = 8
HEAD_SIZE = 128
RANK_LIMIT = 64
ADAPTERS = 32
STEPS = 2
RES = 4
ROWS_DEV = 8
TOKENS = 512
POOL = 32
ROPE_BASE = 500000.0
MESH = pl.DeviceIdType.MESH
F32 = jnp.float32
BF16 = jnp.bfloat16


def dot(a, b):
    return jnp.dot(a, b, preferred_element_type=F32)


def dot_nt(a, b):
    return lax.dot_general(a, b, (((1,), (1,)), ((), ())), preferred_element_type=F32)


def dot_tn(a, b):
    return lax.dot_general(a, b, (((0,), (0,)), ((), ())), preferred_element_type=F32)


def remote(src, dst, send, recv, device):
    return pltpu.make_async_remote_copy(
        src_ref=src, dst_ref=dst, send_sem=send, recv_sem=recv,
        device_id=device, device_id_type=MESH,
    )


def kernel(
    hid, meta, pos_row, pos_col, cos_t, sin_t, lens, pids,
    qw, kt, vt, ow, down, upq, upv, pool,
    out,
    hb, wq, wqp, kvt, wo, pages, dn, uq, uv,
    acc, metap, lowsend, lowrecv, scown, screcv, lift, liftv,
    send1, recv1, qs, kvs, knf, vnf, att, send2, recv2, lhs,
    sb, sf, rh, rf, ta, rah, raf,
    loc, ags, agr, wxs, wxr, fws, fwr, lows, lowr, scs, scr, s1s, s1r, s2s, s2r, rss, rsr,
):
    g = lax.axis_index("group")
    t = lax.axis_index("tensor")
    core = g % 2
    z = t // 16
    y = (t // 4) % 4
    x = t % 4
    zp = 1 - z
    tp = zp * 16 + y * 4 + x
    g2 = (g + 2) % 4
    gs = g + 1 - 2 * core

    def near(along_b, d):
        on_x = (1 - core) * (1 - along_b) + core * along_b
        on_y = 1 - on_x
        xx = (x + 4 + d * on_x) % 4
        yy = (y + 4 + d * on_y) % 4
        return (g, z * 16 + yy * 4 + xx)

    def slice_index(oa, ob):
        dx = oa * (1 - core) + ob * core
        dy = oa * core + ob * (1 - core)
        return ((y + dy) % 4) * 4 + (x + dx) % 4

    half = z * 4096
    local = [
        (qw.at[pl.ds(pl.multiple_of(half, 4096), 4096)], wq),
        (kt.at[:, pl.ds(pl.multiple_of(half, 4096), 4096)], kvt.at[pl.ds(pl.multiple_of(z * 64, 32), 32)]),
        (vt.at[:, pl.ds(pl.multiple_of(half, 4096), 4096)], kvt.at[pl.ds(pl.multiple_of(z * 64 + 32, 32), 32)]),
        (ow.at[:, pl.ds(pl.multiple_of(half, 4096), 4096)], wo.at[z]),
        (down, dn),
        (upq, uq),
        (upv, uv),
        (pool, pages),
    ]
    local = [pltpu.make_async_copy(s, d, loc.at[i]) for i, (s, d) in enumerate(local)]
    local[4].start()
    local[0].start()

    perm = (lax.broadcasted_iota(jnp.int32, (TOKENS, TOKENS), 0) == pos_row[...]).astype(BF16)
    hb[0, 0] = dot(perm, hid[...]).astype(BF16)

    def ag_copy(row, kind):
        along_b = 1 if row else 0
        oa = row - 1

        def at(o, rows=None):
            ref = hb.at[oa, o] if along_b else hb.at[o, 0]
            return ref if rows is None else ref.at[pl.ds(rows, 256)]

        if kind == 0:
            src, dst, d = at(0), at(1), -1
        elif kind == 1:
            src, dst, d = at(0), at(3), 1
        elif kind == 2:
            src, dst, d = at(1, 0), at(2, 0), -1
        else:
            src, dst, d = at(3, 256), at(2, 256), 1
        return remote(src, dst, ags.at[row, kind], agr.at[row, kind], near(along_b, d))

    ag = [[ag_copy(row, kind) for kind in range(4)] for row in range(5)]
    for row in (0, 1):
        for kind in (0, 1):
            ag[row][kind].start()

    def wx_pieces(zq, q, zd):
        c0 = pl.multiple_of(zd * 4096 + q * 1024, 1024)
        d0 = pl.multiple_of(q * 1024, 1024)
        r0 = pl.multiple_of(q * 64, 64)
        return [
            (qw.at[pl.ds(c0, 1024)], wqp.at[pl.ds(d0, 1024)]),
            (kt.at[:, pl.ds(c0, 1024)], kvt.at[pl.ds(pl.multiple_of(zq * 64, 32), 32), pl.ds(d0, 1024)]),
            (vt.at[:, pl.ds(c0, 1024)], kvt.at[pl.ds(pl.multiple_of(zq * 64 + 32, 32), 32), pl.ds(d0, 1024)]),
            (ow.at[pl.ds(r0, 64), pl.ds(pl.multiple_of(zd * 4096, 4096), 4096)], wo.at[zq, pl.ds(r0, 64)]),
        ]

    def wx_copies(i):
        s, d = wx_pieces(z, g, zp)[i]
        return [remote(s, d, wxs.at[i, j], wxr.at[i, j], (gd, tp)) for j, gd in enumerate((g, g2))]

    def wx_arrivals(i):
        res = []
        for j, q in enumerate((g, g2)):
            s, d = wx_pieces(zp, q, z)[i]
            res.append(remote(s, d, wxs.at[i, j], wxr.at[i, j], (g, tp)))
        return res

    def fw_copies(i):
        res = []
        for j, q in enumerate((g, g2)):
            _, d = wx_pieces(zp, q, z)[i]
            res.append(remote(d, d, fws.at[i, j], fwr.at[i, j], (gs, t)))
        return res

    def fw_arrivals(i):
        res = []
        for j, q in enumerate((gs, (gs + 2) % 4)):
            _, d = wx_pieces(zp, q, z)[i]
            res.append(remote(d, d, fws.at[i, j], fwr.at[i, j], (gs, t)))
        return res

    for i in range(4):
        for c in wx_copies(i):
            c.start()
    for i in (1, 2, 5, 6, 3, 7):
        local[i].start()

    metap[...] = dot(perm, meta[...])
    idx = metap[:, :128]
    lane = lax.broadcasted_iota(jnp.int32, (TOKENS, 128), 1)
    idxi = idx.astype(jnp.int32)

    local[4].wait()
    acc[:, :128] = jnp.zeros((TOKENS, 128), F32)

    def low_step(a, carry):
        part = dot(hb[0, 0], dn[a])
        acc[:, :128] = acc[:, :128] + jnp.where(idxi == a, part, 0.0)
        return carry

    lax.fori_loop(0, ADAPTERS, low_step, 0)
    lowsend[...] = acc[:, :128].astype(BF16).reshape(32, 16, 128)

    def low_copy(o):
        d = (t + o) % 32
        return remote(lowsend.at[d], lowrecv.at[t], lows, lowr, (g, d))

    def low_start(o, carry):
        low_copy(o).start()
        return carry

    lax.fori_loop(1, 32, low_start, 0)
    lowrecv[t] = lowsend[t]

    def arrive(row, kind):
        ag[row][kind].wait_recv()

    arrive(0, 0)
    ag[0][2].start()
    ag[2][0].start()
    ag[2][1].start()
    arrive(0, 1)
    ag[0][3].start()
    ag[4][0].start()
    ag[4][1].start()
    arrive(1, 0)
    ag[1][2].start()
    arrive(1, 1)
    ag[1][3].start()

    remote(lowrecv.at[pl.ds(0, 31)], lowrecv.at[pl.ds(0, 31)], lows, lowr, (g, tp)).wait_recv()
    lowrank = jnp.sum(lowrecv[...].astype(F32), axis=0)
    bucket = metap[pl.ds(pl.multiple_of(t * 16, 16), 16), 128:]
    lane16 = lax.broadcasted_iota(jnp.int32, (16, 128), 1) % RANK_LIMIT
    scaled = jnp.where(lane16.astype(F32) < bucket, lowrank * (0.5 * RANK_LIMIT) / bucket, 0.0)
    scown[...] = scaled.astype(BF16)

    def sc_copy(o):
        d = (t + o) % 32
        return remote(scown, screcv.at[t], scs, scr, (g, d))

    def sc_start(o, carry):
        sc_copy(o).start()
        return carry

    lax.fori_loop(1, 32, sc_start, 0)
    screcv[t] = scown[...]

    arrive(0, 2)
    arrive(0, 3)
    ag[3][0].start()
    ag[3][1].start()

    for i in (0, 1, 2):
        local[i].wait()
        for a, c in zip(wx_arrivals(i), fw_copies(i)):
            a.wait_recv()
            c.start()
    for i in (0, 1, 2):
        for a in fw_arrivals(i):
            a.wait_recv()

    acc[...] = jnp.zeros(acc.shape, F32)

    def project(oa, ob):
        k0 = pl.multiple_of(slice_index(oa, ob) * 256, 256)
        h = hb[oa, ob]
        acc[:, 0:256] = acc[:, 0:256] + dot(h, wq[pl.ds(k0, 256)])
        acc[:, 256:512] = acc[:, 256:512] + dot(h, wqp[pl.ds(k0, 256)])
        acc[:, 512:640] = acc[:, 512:640] + dot_nt(h, kvt[:, pl.ds(k0, 256)])

    for o in range(4):
        project(o, 0)
    project(0, 1)
    project(0, 3)

    for oa in (1, 3):
        arrive(1 + oa, 0)
        ag[1 + oa][2].start()
        arrive(1 + oa, 1)
        ag[1 + oa][3].start()
        project(oa, 1)
        project(oa, 3)

    remote(screcv.at[pl.ds(0, 31)], screcv.at[pl.ds(0, 31)], scs, scr, (g, tp)).wait_recv()
    local[5].wait()
    local[6].wait()
    sc = screcv[...].reshape(TOKENS, 128).astype(F32)
    swapped = pltpu.roll(sc, 64, 1)
    sq = jnp.where(lane < 64, sc, swapped).astype(BF16)
    sv = jnp.where(lane < 64, swapped, 0.0).astype(BF16)
    lift[...] = jnp.zeros(lift.shape, F32)

    def lift_step(j, carry):
        mine = jnp.where(idxi == 2 * j + lane // 64, sq.astype(F32), 0.0).astype(BF16)
        lift[...] = lift[...] + dot(mine, uq[pl.ds(pl.multiple_of(j * 128, 128), 128)])
        return carry

    lax.fori_loop(0, ADAPTERS // 2, lift_step, 0)
    liftv[...] = jnp.zeros(liftv.shape, F32)
    svk = sv[:, :64]

    def liftv_step(j, carry):
        part = dot_nt(svk, uv[pl.ds(pl.multiple_of(j * 128, 128), 128)])
        liftv[...] = liftv[...] + jnp.where(idxi == 4 * j + lane // 32, part, 0.0)
        return carry

    lax.fori_loop(0, ADAPTERS // 4, liftv_step, 0)
    lv = liftv[...]
    lv = lv + pltpu.roll(lv, 64, 1)
    lv = lv + pltpu.roll(lv, 32, 1)
    place = lane // 32 == 2 * z + 1
    liftv[...] = jnp.where(place, lv, 0.0)

    arrive(3, 0)
    ag[3][2].start()
    arrive(3, 1)
    ag[3][3].start()
    project(2, 1)
    project(2, 3)
    for oa in (0, 1, 3, 2):
        arrive(1 + oa, 2)
        arrive(1 + oa, 3)
        project(oa, 2)

    def message(v, block):
        m = v.astype(F32).reshape(32, 2, 8, 128)
        for l in range(2):
            send1[l, :, block] = m[:, l].astype(BF16)

    for j in range(2):
        cols = pl.ds(j * 128, 128)
        message(acc[:, j * 128:(j + 1) * 128] + lift[:, j * 128:(j + 1) * 128], 2 * z + j)
        message(acc[:, 256 + j * 128:256 + (j + 1) * 128], 2 * zp + j)
    message(acc[:, 512:640] + liftv[...], 4)

    def s1_copy(l, o):
        d = (t + o) % 32
        return remote(send1.at[l, d], recv1.at[l, t], s1s.at[l], s1r.at[l], ((g + l) % 4, d))

    def s1_start(o, carry):
        s1_copy(1, o).start()
        s1_copy(0, o).start()
        return carry

    lax.fori_loop(1, 32, s1_start, 0)
    s1_copy(1, 0).start()
    recv1[0, t] = send1[0, t]

    local[3].wait()
    for a, c in zip(wx_arrivals(3), fw_copies(3)):
        a.wait_recv()
        c.start()

    local[7].wait()
    remote(recv1.at[0, pl.ds(0, 31)], recv1.at[0, pl.ds(0, 31)], s1s.at[0], s1r.at[0], (g, tp)).wait_recv()
    remote(recv1.at[1], recv1.at[1], s1s.at[1], s1r.at[1], (g, tp)).wait_recv()

    for l in range(2):
        cos8 = cos_t[l * 8:(l + 1) * 8, :][None]
        sin8 = sin_t[l * 8:(l + 1) * 8, :][None]
        for yx in range(16):
            m = recv1[l, yx].astype(F32) + recv1[l, 16 + yx].astype(F32)
            m = m.astype(BF16).astype(F32)
            q = m[:4]
            q = q * cos8 + pltpu.roll(q, 64, 2) * sin8
            for zj in range(4):
                head = (zj // 2) * 32 + yx * 2 + zj % 2
                r0 = l * 512 + head * 8
                qs[r0:r0 + 8, :] = q[zj].astype(BF16).astype(F32)
            yy, xx = yx // 4, yx % 4
            r0 = (l * 4 + yy) * 8
            kvs[r0:r0 + 8, xx * 128:(xx + 1) * 128] = m[4]

    i0 = lax.broadcasted_iota(jnp.int32, (512, 512), 0)
    i1 = lax.broadcasted_iota(jnp.int32, (512, 512), 1)
    target = ((i0 // 32) % 2) * 256 + ((i0 // 64) % 2) * 128 + (i0 // 128) * 32 + i0 % 32
    kvp = dot(kvs[...].astype(BF16), (target == i1).astype(BF16))
    for l in range(2):
        cos8 = cos_t[l * 8:(l + 1) * 8, :]
        sin8 = sin_t[l * 8:(l + 1) * 8, :]
        for yy in range(4):
            r0 = (l * 4 + yy) * 8
            for zz in range(2):
                k = kvp[r0:r0 + 8, zz * 128:(zz + 1) * 128]
                k = k * cos8 + pltpu.roll(k, 64, 1) * sin8
                n = zz * 4 + yy
                knf[l * 8:(l + 1) * 8, n * 128:(n + 1) * 128] = k
                vnf[l * 8:(l + 1) * 8, n * 128:(n + 1) * 128] = kvp[r0:r0 + 8, 256 + zz * 128:256 + (zz + 1) * 128]
    knew = knf[...].astype(BF16)
    vnew = vnf[...].astype(BF16)

    head_of = lax.broadcasted_iota(jnp.int32, (128, 128), 0) % 64
    pos = lax.broadcasted_iota(jnp.int32, (272, 128), 0)
    step = lax.broadcasted_iota(jnp.int32, (272, 128), 1) // 64

    def attend(i, carry):
        l = i // 4
        ii = i % 4
        base = l * 512 + 2 * ii
        q = jnp.concatenate([qs[pl.ds(base + s, 64, stride=8), :] for s in range(2)], axis=0)
        bd = jnp.concatenate(
            [jnp.where(head_of // 8 == n, q, 0.0).astype(BF16) for n in range(8)], axis=1
        )
        keys = jnp.concatenate([pages[pids[i, j], :, :1024] for j in range(4)] + [knew], axis=0)
        values = jnp.concatenate([pages[pids[i, j], :, 1024:] for j in range(4)] + [vnew], axis=0)
        scores = dot_nt(keys, bd) * HEAD_SIZE ** (-0.5)
        first = 256 + 2 * i
        usable = (pos < lens[i]) | (pos == first) | ((pos == first + 1) & (step == 1))
        top = jnp.max(jnp.where(usable, scores, -jnp.inf), axis=0, keepdims=True)
        e = jnp.where(usable, jnp.exp(scores - top), 0.0)
        p = (e / jnp.sum(e, axis=0, keepdims=True)).astype(BF16)
        o = dot_tn(p, values)
        for s in range(2):
            for n in range(8):
                att[pl.ds(pl.multiple_of((2 * i + s) * 64 + n * 8, 8), 8), :] = o[
                    s * 64 + n * 8:s * 64 + (n + 1) * 8, n * 128:(n + 1) * 128
                ]
        return carry

    lax.fori_loop(0, 8, attend, 0)

    def pack2(yx, carry):
        for l in range(2):
            for zj in range(4):
                head = (zj // 2) * 32 + yx * 2 + zj % 2
                send2[l, yx, zj] = att[pl.ds(l * 512 + head, 8, stride=64), :].astype(BF16)
        return carry

    lax.fori_loop(0, 16, pack2, 0)

    def s2_copy(l, o):
        d = (t + o) % 32
        return remote(send2.at[l, d % 16], recv2.at[l, t], s2s.at[l], s2r.at[l], ((g + 4 - l) % 4, d))

    def s2_start(o, carry):
        s2_copy(1, o).start()
        s2_copy(0, o).start()
        return carry

    lax.fori_loop(1, 32, s2_start, 0)
    s2_copy(1, 0).start()
    recv2[0, t] = send2[0, t % 16]

    for a in fw_arrivals(3):
        a.wait_recv()
    remote(recv2.at[0, pl.ds(0, 31)], recv2.at[0, pl.ds(0, 31)], s2s.at[0], s2r.at[0], (g, tp)).wait_recv()
    remote(recv2.at[1], recv2.at[1], s2s.at[1], s2r.at[1], (g, tp)).wait_recv()

    def build(s, carry):
        r0 = pl.multiple_of(s * 16, 16)
        for zj in range(4):
            both = jnp.concatenate([recv2[l, s, zj].astype(F32) for l in range(2)], axis=0)
            lhs[pl.ds(r0, 16), zj * 128:(zj + 1) * 128] = both.astype(BF16)
        return carry

    lax.fori_loop(0, 32, build, 0)

    def partial(oa, ob):
        c0 = pl.multiple_of(slice_index(oa, ob) * 256, 256)
        return dot(lhs[:, :256], wo[0, :, pl.ds(c0, 256)]) + dot(lhs[:, 256:], wo[1, :, pl.ds(c0, 256)])

    def rs_copy(row, kind):
        along_b = 1 if row else 0
        oa = row - 1

        def src(o, rows=None):
            ref = sb.at[oa, o] if along_b else ta.at[o]
            return ref if rows is None else ref.at[pl.ds(rows, 256)]

        halves = rh.at[oa] if along_b else rah
        fulls = rf.at[oa] if along_b else raf
        if kind == 0:
            s, d, way = src(2, 0), halves.at[0], -1
        elif kind == 1:
            s, d, way = src(2, 256), halves.at[1], 1
        elif kind == 2:
            s, d, way = src(3), fulls.at[0], -1
        else:
            s, d, way = src(1), fulls.at[1], 1
        return remote(s, d, rss.at[row, kind], rsr.at[row, kind], near(along_b, way))

    rs = [[rs_copy(row, kind) for kind in range(4)] for row in range(5)]
    order = (2, 1, 3, 0)
    for oa in order:
        sb[oa, 2] = partial(oa, 2).astype(BF16)
        rs[1 + oa][0].start()
        rs[1 + oa][1].start()
    for oa in order:
        sf[oa, 2] = partial(oa, 3)
        rs[1 + oa][0].wait_recv()
        sb[oa, 3, 0:256] = (sf[oa, 2, 0:256] + rh[oa, 0].astype(F32)).astype(BF16)
        sb[oa, 3, 256:512] = sf[oa, 2, 256:512].astype(BF16)
        rs[1 + oa][2].start()
        sf[oa, 1] = partial(oa, 1)
        rs[1 + oa][1].wait_recv()
        sb[oa, 1, 0:256] = sf[oa, 1, 0:256].astype(BF16)
        sb[oa, 1, 256:512] = (sf[oa, 1, 256:512] + rh[oa, 1].astype(F32)).astype(BF16)
        rs[1 + oa][3].start()
    for oa in order:
        sf[oa, 0] = partial(oa, 0)

    def total(oa):
        rs[1 + oa][2].wait_recv()
        rs[1 + oa][3].wait_recv()
        return sf[oa, 0] + rf[oa, 0].astype(F32) + rf[oa, 1].astype(F32)

    ta[2] = total(2).astype(BF16)
    rs[0][0].start()
    rs[0][1].start()
    sf[1, 0] = total(1)
    rs[0][1].wait_recv()
    ta[1, 0:256] = sf[1, 0, 0:256].astype(BF16)
    ta[1, 256:512] = (sf[1, 0, 256:512] + rah[1].astype(F32)).astype(BF16)
    rs[0][3].start()
    sf[3, 0] = total(3)
    rs[0][0].wait_recv()
    ta[3, 0:256] = (sf[3, 0, 0:256] + rah[0].astype(F32)).astype(BF16)
    ta[3, 256:512] = sf[3, 0, 256:512].astype(BF16)
    rs[0][2].start()
    sf[0, 0] = total(0)
    rs[0][2].wait_recv()
    rs[0][3].wait_recv()
    final = (sf[0, 0] + raf[0].astype(F32) + raf[1].astype(F32)).astype(BF16)
    back = (lax.broadcasted_iota(jnp.int32, (TOKENS, TOKENS), 1) == pos_col[...]).astype(BF16)
    out[...] = dot(back, final).astype(BF16)

    for row in range(5):
        for kind in range(4):
            ag[row][kind].wait_send()
            rs[row][kind].wait_send()
    for i in range(4):
        for c in wx_copies(i) + fw_copies(i):
            c.wait_send()
    remote(lowrecv.at[pl.ds(0, 31)], lowrecv.at[pl.ds(0, 31)], lows, lowr, (g, tp)).wait_send()
    remote(screcv.at[pl.ds(0, 31)], screcv.at[pl.ds(0, 31)], scs, scr, (g, tp)).wait_send()
    remote(recv1.at[0, pl.ds(0, 31)], recv1.at[0, pl.ds(0, 31)], s1s.at[0], s1r.at[0], (g, tp)).wait_send()
    remote(recv1.at[1], recv1.at[1], s1s.at[1], s1r.at[1], (g, tp)).wait_send()
    remote(recv2.at[0, pl.ds(0, 31)], recv2.at[0, pl.ds(0, 31)], s2s.at[0], s2r.at[0], (g, tp)).wait_send()
    remote(recv2.at[1], recv2.at[1], s2s.at[1], s2r.at[1], (g, tp)).wait_send()


def scratch():
    v = pltpu.VMEM
    dma = pltpu.SemaphoreType.DMA
    return [
        v((4, 4, 512, 256), BF16),
        v((4096, 256), BF16),
        v((4096, 256), BF16),
        v((128, 4096), BF16),
        v((2, 256, 4096), BF16),
        v((32, 64, 2048), BF16),
        v((32, 256, 128), BF16),
        v((2048, 256), BF16),
        v((1024, 64), BF16),
        v((512, 640), F32),
        v((512, 256), F32),
        v((32, 16, 128), BF16),
        v((32, 16, 128), BF16),
        v((16, 128), BF16),
        v((32, 16, 128), BF16),
        v((512, 256), F32),
        v((512, 128), F32),
        v((2, 32, 5, 8, 128), BF16),
        v((2, 32, 5, 8, 128), BF16),
        v((1024, 128), F32),
        v((64, 512), F32),
        v((16, 1024), F32),
        v((16, 1024), F32),
        v((1024, 128), F32),
        v((2, 16, 4, 8, 128), BF16),
        v((2, 32, 4, 8, 128), BF16),
        v((512, 512), BF16),
        v((4, 4, 512, 256), BF16),
        v((4, 3, 512, 256), F32),
        v((4, 2, 256, 256), BF16),
        v((4, 2, 512, 256), BF16),
        v((4, 512, 256), BF16),
        v((2, 256, 256), BF16),
        v((2, 512, 256), BF16),
        dma((8,)),
        dma((5, 4)), dma((5, 4)),
        dma((4, 2)), dma((4, 2)),
        dma((4, 2)), dma((4, 2)),
        dma, dma, dma, dma,
        dma((2,)), dma((2,)),
        dma((2,)), dma((2,)),
        dma((5, 4)), dma((5, 4)),
    ]


def local(
    hidden, query_weight, key_weight, value_weight, output_weight, adapter_down_maps,
    adapter_up_query, adapter_up_value, key_value_pages, row_adapter_index,
    row_rank_bucket, lengths, row_page_index,
):
    g = lax.axis_index("group")
    t = lax.axis_index("tensor")
    i32 = jnp.int32

    table = lax.dynamic_slice_in_dim(row_page_index, g * 256, 256, 0)
    block = jnp.arange(256, dtype=i32) // ROWS_DEV
    flags = (table[:, 0] // POOL != g * 32 + block).astype(i32).reshape(32, 8)
    earlier = (jnp.arange(8)[:, None] > jnp.arange(8)[None, :]).astype(i32)

    def places(f):
        before = jnp.sum(earlier * f[..., None, :], axis=-1)
        return jnp.where(f == 1, RES + before, jnp.arange(8, dtype=i32) - before)

    place = places(flags).reshape(256)
    pos = (block * 16 + place * 2)[:, None] + jnp.arange(STEPS, dtype=i32)[None, :]
    pos = pos.reshape(TOKENS)

    base = (g * 32 + t) * POOL
    lens, pids = [], []
    for l in range(2):
        gg = (g + 4 - l) % 4
        first = gg * 256 + t * ROWS_DEV
        tab = lax.dynamic_slice_in_dim(row_page_index, first, ROWS_DEV, 0)
        lng = lax.dynamic_slice_in_dim(lengths, first, ROWS_DEV, 0)
        pl8 = places((tab[:, 0] // POOL != gg * 32 + t).astype(i32))
        sel = (pl8[None, :] == l * RES + jnp.arange(4, dtype=i32)[:, None]).astype(i32)
        lens.append(jnp.sum(sel * lng[None, :], axis=1))
        pids.append(jnp.sum(sel[:, :, None] * tab[None], axis=1))
    lens = jnp.concatenate(lens)
    pids = jnp.clip(jnp.concatenate(pids) - base, 0, POOL - 1)
    positions = (lens[:, None] + jnp.arange(STEPS, dtype=i32)[None, :]).reshape(16)
    inverse_freq = jnp.exp(-math.log(ROPE_BASE) * jnp.arange(64, dtype=F32) / 64)
    angles = positions.astype(F32)[:, None] * jnp.concatenate([inverse_freq, inverse_freq])[None]
    cos_t = jnp.cos(angles)
    sin_t = jnp.sin(angles) * jnp.where(jnp.arange(128) < 64, -1.0, 1.0)[None]

    meta = jnp.stack([row_adapter_index, row_rank_bucket], axis=1).astype(BF16)
    meta = jnp.broadcast_to(meta[:, None, :, None], (256, STEPS, 2, 128)).reshape(TOKENS, 256)

    vm = pl.BlockSpec(memory_space=pltpu.VMEM)
    sm = pl.BlockSpec(memory_space=pltpu.SMEM)
    hbm = pl.BlockSpec(memory_space=pl.ANY)
    res = pl.pallas_call(
        kernel,
        out_shape=jax.ShapeDtypeStruct((TOKENS, 256), BF16),
        in_specs=[vm] * 6 + [sm] * 2 + [hbm] * 8,
        out_specs=vm,
        scratch_shapes=scratch(),
        compiler_params=pltpu.CompilerParams(
            has_side_effects=True, vmem_limit_bytes=60 * 1024 * 1024
        ),
    )(
        hidden.reshape(TOKENS, 256), meta, pos[None, :], pos[:, None], cos_t, sin_t, lens, pids,
        query_weight, key_weight.T, value_weight.T, output_weight, adapter_down_maps,
        adapter_up_query.reshape(2048, 256),
        adapter_up_value.transpose(0, 2, 1).reshape(1024, 64), key_value_pages,
    )
    return res.reshape(256, STEPS, 256)


def solution(mesh):
    in_specs = (
        P("group", None, "tensor"),
        P(None, "tensor"),
        P(None, "tensor"),
        P(None, "tensor"),
        P("tensor", None),
        P(None, "tensor", None),
        P(None, None, "tensor"),
        P(None, None, "tensor"),
        P(("group", "tensor"), None, None),
        P("group"),
        P("group"),
        P(),
        P(),
    )
    out_specs = P("group", None, "tensor")
    return jax.shard_map(local, mesh=mesh, in_specs=in_specs, out_specs=out_specs, check_vma=False)
```

time: 677 us -> 131 us (0.19)
  waiting for transfers between devices: 436 us -> 0 us
  local copies, waits for them, and re-layouts: 127 us -> 9.12 us
  Pallas kernels: 0 us -> 115 us
  matrix products: 44.9 us -> 0 us
  starting transfers between devices: 25.4 us -> 0 us
  between operations: 13.5 us -> 0.08 us
  blocking collectives: 12.8 us -> 0 us
  other arithmetic: 14.8 us -> 4.79 us
    reduce_scatter x1 -> x0, waiting for transfers between devices: 179 us -> none  [local(): lax.psum_scatter(partial_out.astype(jnp.bfloat16), 'tensor', scatter_dime...]
    all_gather x2 -> x0, waiting for transfers between devices: 157 us -> none  [the longest x1 156 us: local(): lax.all_gather(hidden, 'tensor', axis=2, tiled=True)]
    pallas_call x0 -> x1, Pallas kernels: none -> 115 us  [local(): pl.pallas_call(kernel, out_shape=jax.ShapeDtypeStruct((TOKENS, 256), BF16...]
    ppermute x1 -> x0, waiting for transfers between devices: 89.9 us -> none  [from_behind(): return lax.ppermute(block, axis, route)]
    dot_general x9 -> x0, matrix products: 44.9 us -> none  [the longest x1 7.76 us: local(): jnp.dot(returned.reshape(group_rows * step_count, -1), output_weight, pre...]
    gather x7 -> x0, local copies, waits for them, and re-layouts: 42.4 us -> none  [the longest x1 9.62 us: local(): row_down_maps = adapter_down_maps[row_adapter_index]]
    all_to_all x3 -> x0, starting transfers between devices: 21.9 us -> none  [the longest x1 8.04 us: local(): lax.all_to_all(query_rows, 'tensor', split_axis=0, concat_axis=2, tiled=T...]
    slice x6 -> x1, local copies, waits for them, and re-layouts: 17.1 us -> 0.71 us  [local(): flags = (table[:, 0] // POOL != g * 32 + block).astype(i32).reshape(32, 8)]
  transfers between devices with their start and end apart: 7 -> 0, of which waited for: 7 -> 0; matrix products, arithmetic and copies ran while one was open for 16% -> 0% of each run, Pallas kernels for 0% -> 0%
where the time goes in v1:
time: 131 us; the launch traced here: 129 us
  Pallas kernels  115 us (88%)
  local copies, waits for them, and re-layouts  9.12 us (7%)
  other arithmetic  4.79 us (4%)
    pallas_call x1, Pallas kernels, local(): pl.pallas_call(kernel, out_shape=jax.ShapeDtypeStruct((TOKENS, 256), BF16...  115 us

profile of v1, /device:TPU:0, one launch (start us, length us, event | category | flops | bytes accessed | tf_op | source)
XLA Modules:
  0.0 129.3 jit_solution(1734144351593929543)
XLA Ops:
  0.0 0.7 convert.8
  0.7 0.7 convert.9
  1.5 0.7 fusion.13
  2.2 0.8 fusion.14
  3.0 0.8 constant_dynamic-slice_fusion.1
  3.8 0.1 select_reduce_fusion
  3.9 0.2 fusion.11
  4.1 0.1 select_reduce_fusion.1
  4.2 0.1 select_reduce_fusion.2
  4.5 0.2 multiply_reduce_fusion.1
  4.7 0.1 multiply_reduce_fusion.2
  4.8 0.6 fusion.5.pids
  5.6 0.7 fusion
  6.8 0.1 add.226
  6.9 0.7 multiply_add_fusion.1
  7.6 0.1 copy.25
  7.8 0.1 iota_add_fusion
  7.9 0.7 add.232.pos_row
  8.6 0.8 add.250.pos_col
  9.4 0.3 broadcast_in_dim.8
  9.8 0.7 copy.35
  10.5 1.8 %reshape.414.hid = bf16[512,256]{1,0:T(8,128)(2,1)} reshape(bf16[256,2,256]{2,1,0:T(2,128)(2,1)} %param.13) | data formatting | bytes 524288 | tf_op jit(solution)/shard_map/reshape | solution.py:623
  12.2 115.3 %shard_map.127 = bf16[512,256]{1,0:T(8,128)(2,1)} custom-call(bf16[512,256]{1,0:T(8,128)(2,1)} %reshape.414.hid, bf16[512,256]{1,0:T(8,128)(2,1)} %bitcast.32, s32[1,512]{1,0:T(1,128)} %add.232.pos_row, s32[512,1]{1,0:T(8,128)} %add.250.pos_col, f32[16,128]{1,0:T(8,128)} %get-tuple-element.12.cos_t, f32[16,128]{1,0:T(8,128)} %get-tuple-element.11.sin_t, ...), custom_call_target="tpu_custom_call" | custom-call | tf_op jit(solution)/shard_map/pallas_call | solution.py:613
  127.5 1.8 %reshape.418 = bf16[256,2,256]{2,1,0:T(2,128)(2,1)} reshape(bf16[512,256]{1,0:T(8,128)(2,1)} %shard_map.127) | data formatting | bytes 524288 | tf_op jit(solution)/shard_map/reshape | solution.py:628
  (25 shorter events, 1.0 us)
Async XLA Ops:
  4.4 7.8 %copy-start = (s32[8]{0:T(128)}, s32[8]{0:T(128)S(1)}, u32[]{:S(2)}) copy-start(s32[8]{0:T(128)S(1)} %pad_add_fusion.lens) | copy-start | bytes 100

commit v2 on v1

--- a/solution.py
+++ b/solution.py
@@ -3,6 +3,7 @@
 
 import jax
 import jax.numpy as jnp
+import numpy as np
 from jax import lax
 from jax.experimental import pallas as pl
 from jax.experimental.pallas import tpu as pltpu
@@ -44,14 +45,15 @@
 
 
 def kernel(
-    hid, meta, pos_row, pos_col, cos_t, sin_t, lens, pids,
+    hid, adapters, buckets, table_v, cos_tab, sin_tab, lengths, table,
     qw, kt, vt, ow, down, upq, upv, pool,
     out,
     hb, wq, wqp, kvt, wo, pages, dn, uq, uv,
+    cos_t, sin_t, lens, pids, back,
     acc, metap, lowsend, lowrecv, scown, screcv, lift, liftv,
     send1, recv1, qs, kvs, knf, vnf, att, send2, recv2, lhs,
     sb, sf, rh, rf, ta, rah, raf,
-    loc, ags, agr, wxs, wxr, fws, fwr, lows, lowr, scs, scr, s1s, s1r, s2s, s2r, rss, rsr,
+    loc, ags, agr, wxs, wxr, fws, fwr, lows, lowr, scs, scr, s1s, s1r, s2s, s2r, rss, rsr, plane_sem, all_sem,
 ):
     g = lax.axis_index("group")
     t = lax.axis_index("tensor")
@@ -91,7 +93,44 @@
     local[4].start()
     local[0].start()
 
-    perm = (lax.broadcasted_iota(jnp.int32, (TOKENS, TOKENS), 0) == pos_row[...]).astype(BF16)
+    barrier = pltpu.get_barrier_semaphore()
+
+    def ring_x(d):
+        return (g, z * 16 + y * 4 + (x + d) % 4)
+
+    def ring_y(d):
+        return (g, z * 16 + ((y + d) % 4) * 4 + x)
+
+    def line_z(d):
+        zz = (2 * (g // 2) + z + d // 2) % 4
+        return ((zz // 2) * 2 + (core + d) % 2, (zz % 2) * 16 + y * 4 + x)
+
+    def greet(sem, device):
+        pl.semaphore_signal(sem, inc=1, device_id=device, device_id_type=MESH)
+
+    for d in range(1, 4):
+        greet(barrier, ring_x(d))
+        greet(barrier, ring_y(d))
+    for d in range(1, 8):
+        greet(barrier, line_z(d))
+
+    def iota(shape, dim):
+        return lax.broadcasted_iota(jnp.int32, shape, dim)
+
+    tok = iota((8, TOKENS), 1)
+    spread = (iota((256, TOKENS), 0) == iota((256, TOKENS), 1) // 2).astype(BF16)
+    ahead = (
+        (iota((256, TOKENS), 0) // 8 == iota((256, TOKENS), 1) // 16)
+        & (iota((256, TOKENS), 0) < iota((256, TOKENS), 1) // 2)
+    ).astype(BF16)
+    first_page = table_v[0:1, pl.ds(pl.multiple_of(g * 256, 256), 256)]
+    moved = (first_page // POOL != g * 32 + iota((1, 256), 1) // 8).astype(F32)
+    moved = jnp.broadcast_to(moved, (8, 256)).astype(BF16)
+    resumed = dot(moved, spread).astype(jnp.int32)
+    before = dot(moved, ahead).astype(jnp.int32)
+    place = jnp.where(resumed == 1, before, (tok // 2) % 8 - before)
+    pos = resumed * 256 + (tok // 16) * 8 + place * 2 + tok % 2
+    perm = (iota((TOKENS, TOKENS), 0) == pos[0:1]).astype(BF16)
     hb[0, 0] = dot(perm, hid[...]).astype(BF16)
 
     def ag_copy(row, kind):
@@ -113,9 +152,12 @@
         return remote(src, dst, ags.at[row, kind], agr.at[row, kind], near(along_b, d))
 
     ag = [[ag_copy(row, kind) for kind in range(4)] for row in range(5)]
+    pl.semaphore_wait(barrier, 13)
     for row in (0, 1):
         for kind in (0, 1):
             ag[row][kind].start()
+    for d in range(1, 4):
+        greet(plane_sem, ring_y(d))
 
     def wx_pieces(zq, q, zd):
         c0 = pl.multiple_of(zd * 4096 + q * 1024, 1024)
@@ -159,7 +201,38 @@
     for i in (1, 2, 5, 6, 3, 7):
         local[i].start()
 
-    metap[...] = dot(perm, meta[...])
+    def along(row):
+        wide = jnp.broadcast_to(row.astype(F32), (128, 256)).astype(BF16)
+        return dot_nt(perm, dot(wide, spread).astype(BF16))
+
+    metap[:, :128] = along(adapters[...])
+    metap[:, 128:] = along(buckets[...])
+    pl.semaphore_wait(plane_sem, 3)
+    for d in range(1, 8):
+        greet(all_sem, line_z(d))
+    eye = (iota((TOKENS, TOKENS), 0) == iota((TOKENS, TOKENS), 1)).astype(BF16)
+    back[...] = dot_nt(eye, perm).astype(BF16)
+
+    base = (g * 32 + t) * POOL
+    for l in range(2):
+        gg = (g + 4 - l) % 4
+        first = gg * 256 + t * ROWS_DEV
+        marks, spots = [], []
+        count = jnp.int32(0)
+        for k in range(ROWS_DEV):
+            mark = jnp.where(table[0, first + k] // POOL != gg * 32 + t, 1, 0)
+            marks.append(mark)
+            spots.append(jnp.where(mark == 1, count, k - count))
+            count = count + mark
+        for i in range(RES):
+            mine = [(marks[k] == l) & (spots[k] == i) for k in range(ROWS_DEV)]
+            row = l * RES + i
+            lens[row] = sum(jnp.where(mine[k], lengths[first + k], 0) for k in range(ROWS_DEV))
+            for j in range(4):
+                page = sum(jnp.where(mine[k], table[j, first + k], 0) for k in range(ROWS_DEV))
+                pids[row, j] = jnp.clip(page - base, 0, POOL - 1)
+            cos_t[2 * row:2 * row + 2, :] = cos_tab[pl.ds(lens[row], 2), :]
+            sin_t[2 * row:2 * row + 2, :] = sin_tab[pl.ds(lens[row], 2), :]
     idx = metap[:, :128]
     lane = lax.broadcasted_iota(jnp.int32, (TOKENS, 128), 1)
     idxi = idx.astype(jnp.int32)
@@ -173,7 +246,9 @@
         return carry
 
     lax.fori_loop(0, ADAPTERS, low_step, 0)
-    lowsend[...] = acc[:, :128].astype(BF16).reshape(32, 16, 128)
+    for l in range(2):
+        lowsend[:, l] = acc[l * 256:(l + 1) * 256, :128].reshape(32, 8, 128).astype(BF16)
+    pl.semaphore_wait(all_sem, 7)
 
     def low_copy(o):
         d = (t + o) % 32
@@ -203,11 +278,12 @@
     ag[1][3].start()
 
     remote(lowrecv.at[pl.ds(0, 31)], lowrecv.at[pl.ds(0, 31)], lows, lowr, (g, tp)).wait_recv()
-    lowrank = jnp.sum(lowrecv[...].astype(F32), axis=0)
-    bucket = metap[pl.ds(pl.multiple_of(t * 16, 16), 16), 128:]
-    lane16 = lax.broadcasted_iota(jnp.int32, (16, 128), 1) % RANK_LIMIT
-    scaled = jnp.where(lane16.astype(F32) < bucket, lowrank * (0.5 * RANK_LIMIT) / bucket, 0.0)
-    scown[...] = scaled.astype(BF16)
+    lane16 = lax.broadcasted_iota(jnp.int32, (8, 128), 1) % RANK_LIMIT
+    for l in range(2):
+        lowrank = jnp.sum(lowrecv[:, l].astype(F32), axis=0)
+        bucket = metap[pl.ds(pl.multiple_of(l * 256 + t * 8, 8), 8), 128:]
+        scaled = jnp.where(lane16.astype(F32) < bucket, lowrank * (0.5 * RANK_LIMIT) / bucket, 0.0)
+        scown[l] = scaled.astype(BF16)
 
     def sc_copy(o):
         d = (t + o) % 32
@@ -259,7 +335,7 @@
     remote(screcv.at[pl.ds(0, 31)], screcv.at[pl.ds(0, 31)], scs, scr, (g, tp)).wait_recv()
     local[5].wait()
     local[6].wait()
-    sc = screcv[...].reshape(TOKENS, 128).astype(F32)
+    sc = jnp.concatenate([screcv[:, l].astype(F32).reshape(256, 128) for l in range(2)], axis=0)
     swapped = pltpu.roll(sc, 64, 1)
     sq = jnp.where(lane < 64, sc, swapped).astype(BF16)
     sv = jnp.where(lane < 64, swapped, 0.0).astype(BF16)
@@ -298,9 +374,9 @@
         project(oa, 2)
 
     def message(v, block):
-        m = v.astype(F32).reshape(32, 2, 8, 128)
+        m = v.reshape(2, 32, 8, 128)
         for l in range(2):
-            send1[l, :, block] = m[:, l].astype(BF16)
+            send1[l, :, block] = m[l].astype(BF16)
 
     for j in range(2):
         cols = pl.ds(j * 128, 128)
@@ -392,7 +468,7 @@
                 ]
         return carry
 
-    lax.fori_loop(0, 8, attend, 0)
+    lax.fori_loop(0, 8, attend, 0, unroll=2)
 
     def pack2(yx, carry):
         for l in range(2):
@@ -422,13 +498,14 @@
     remote(recv2.at[1], recv2.at[1], s2s.at[1], s2r.at[1], (g, tp)).wait_recv()
 
     def build(s, carry):
-        r0 = pl.multiple_of(s * 16, 16)
-        for zj in range(4):
-            both = jnp.concatenate([recv2[l, s, zj].astype(F32) for l in range(2)], axis=0)
-            lhs[pl.ds(r0, 16), zj * 128:(zj + 1) * 128] = both.astype(BF16)
-        return carry
-
-    lax.fori_loop(0, 32, build, 0)
+        for l in range(2):
+            r0 = pl.multiple_of(l * 256 + s * 16, 16)
+            for zj in range(4):
+                both = jnp.concatenate([recv2[l, 2 * s + h, zj].astype(F32) for h in range(2)], axis=0)
+                lhs[pl.ds(r0, 16), zj * 128:(zj + 1) * 128] = both.astype(BF16)
+        return carry
+
+    lax.fori_loop(0, 16, build, 0)
 
     def partial(oa, ob):
         c0 = pl.multiple_of(slice_index(oa, ob) * 256, 256)
@@ -496,8 +573,7 @@
     rs[0][2].wait_recv()
     rs[0][3].wait_recv()
     final = (sf[0, 0] + raf[0].astype(F32) + raf[1].astype(F32)).astype(BF16)
-    back = (lax.broadcasted_iota(jnp.int32, (TOKENS, TOKENS), 1) == pos_col[...]).astype(BF16)
-    out[...] = dot(back, final).astype(BF16)
+    out[...] = dot(back[...], final).astype(BF16)
 
     for row in range(5):
         for kind in range(4):
@@ -527,12 +603,17 @@
         v((32, 256, 128), BF16),
         v((2048, 256), BF16),
         v((1024, 64), BF16),
+        v((16, 128), F32),
+        v((16, 128), F32),
+        pltpu.SMEM((8,), jnp.int32),
+        pltpu.SMEM((8, 4), jnp.int32),
+        v((512, 512), BF16),
         v((512, 640), F32),
         v((512, 256), F32),
-        v((32, 16, 128), BF16),
-        v((32, 16, 128), BF16),
-        v((16, 128), BF16),
-        v((32, 16, 128), BF16),
+        v((32, 2, 8, 128), BF16),
+        v((32, 2, 8, 128), BF16),
+        v((2, 8, 128), BF16),
+        v((32, 2, 8, 128), BF16),
         v((512, 256), F32),
         v((512, 128), F32),
         v((2, 32, 5, 8, 128), BF16),
@@ -560,6 +641,8 @@
         dma((2,)), dma((2,)),
         dma((2,)), dma((2,)),
         dma((5, 4)), dma((5, 4)),
+        pltpu.SemaphoreType.REGULAR,
+        pltpu.SemaphoreType.REGULAR,
     ]
 
 
@@ -568,44 +651,12 @@
     adapter_up_query, adapter_up_value, key_value_pages, row_adapter_index,
     row_rank_bucket, lengths, row_page_index,
 ):
-    g = lax.axis_index("group")
-    t = lax.axis_index("tensor")
-    i32 = jnp.int32
-
-    table = lax.dynamic_slice_in_dim(row_page_index, g * 256, 256, 0)
-    block = jnp.arange(256, dtype=i32) // ROWS_DEV
-    flags = (table[:, 0] // POOL != g * 32 + block).astype(i32).reshape(32, 8)
-    earlier = (jnp.arange(8)[:, None] > jnp.arange(8)[None, :]).astype(i32)
-
-    def places(f):
-        before = jnp.sum(earlier * f[..., None, :], axis=-1)
-        return jnp.where(f == 1, RES + before, jnp.arange(8, dtype=i32) - before)
-
-    place = places(flags).reshape(256)
-    pos = (block * 16 + place * 2)[:, None] + jnp.arange(STEPS, dtype=i32)[None, :]
-    pos = pos.reshape(TOKENS)
-
-    base = (g * 32 + t) * POOL
-    lens, pids = [], []
-    for l in range(2):
-        gg = (g + 4 - l) % 4
-        first = gg * 256 + t * ROWS_DEV
-        tab = lax.dynamic_slice_in_dim(row_page_index, first, ROWS_DEV, 0)
-        lng = lax.dynamic_slice_in_dim(lengths, first, ROWS_DEV, 0)
-        pl8 = places((tab[:, 0] // POOL != gg * 32 + t).astype(i32))
-        sel = (pl8[None, :] == l * RES + jnp.arange(4, dtype=i32)[:, None]).astype(i32)
-        lens.append(jnp.sum(sel * lng[None, :], axis=1))
-        pids.append(jnp.sum(sel[:, :, None] * tab[None], axis=1))
-    lens = jnp.concatenate(lens)
-    pids = jnp.clip(jnp.concatenate(pids) - base, 0, POOL - 1)
-    positions = (lens[:, None] + jnp.arange(STEPS, dtype=i32)[None, :]).reshape(16)
-    inverse_freq = jnp.exp(-math.log(ROPE_BASE) * jnp.arange(64, dtype=F32) / 64)
-    angles = positions.astype(F32)[:, None] * jnp.concatenate([inverse_freq, inverse_freq])[None]
-    cos_t = jnp.cos(angles)
-    sin_t = jnp.sin(angles) * jnp.where(jnp.arange(128) < 64, -1.0, 1.0)[None]
-
-    meta = jnp.stack([row_adapter_index, row_rank_bucket], axis=1).astype(BF16)
-    meta = jnp.broadcast_to(meta[:, None, :, None], (256, STEPS, 2, 128)).reshape(TOKENS, 256)
+    positions = np.arange(264, dtype=np.float32)
+    inverse_freq = np.exp(np.float32(-math.log(ROPE_BASE)) * np.arange(64, dtype=np.float32) / np.float32(64))
+    angles = positions[:, None] * np.concatenate([inverse_freq, inverse_freq])[None].astype(np.float32)
+    sign = np.where(np.arange(128) < 64, -1.0, 1.0)[None]
+    cos_tab = jnp.asarray(np.cos(angles), F32)
+    sin_tab = jnp.asarray(np.sin(angles) * sign, F32)
 
     vm = pl.BlockSpec(memory_space=pltpu.VMEM)
     sm = pl.BlockSpec(memory_space=pltpu.SMEM)
@@ -617,10 +668,11 @@
         out_specs=vm,
         scratch_shapes=scratch(),
         compiler_params=pltpu.CompilerParams(
-            has_side_effects=True, vmem_limit_bytes=60 * 1024 * 1024
+            collective_id=0, has_side_effects=True, vmem_limit_bytes=60 * 1024 * 1024
         ),
     )(
-        hidden.reshape(TOKENS, 256), meta, pos[None, :], pos[:, None], cos_t, sin_t, lens, pids,
+        hidden.reshape(TOKENS, 256), row_adapter_index[None, :], row_rank_bucket[None, :], row_page_index.T,
+        cos_tab, sin_tab, lengths, row_page_index.T,
         query_weight, key_weight.T, value_weight.T, output_weight, adapter_down_maps,
         adapter_up_query.reshape(2048, 256),
         adapter_up_value.transpose(0, 2, 1).reshape(1024, 64), key_value_pages,

time: 131 us -> 112 us (0.85)
  Pallas kernels: 115 us -> 108 us
  local copies, waits for them, and re-layouts: 9.12 us -> 3.5 us
  other arithmetic: 4.79 us -> 0 us
    pallas_call x1, Pallas kernels: 115 us -> 108 us  [local(): pl.pallas_call(kernel, out_shape=jax.ShapeDtypeStruct((TOKENS, 256), BF16...]
    add x4 -> x0, local copies, waits for them, and re-layouts: 1.69 us -> none  [the longest x2 1.52 us: local(): (block * 16 + place * 2)[:, None] + jnp.arange(STEPS, dtype=i32)[None, :]]
    dynamic_slice x2 -> x0, local copies, waits for them, and re-layouts: 1.61 us -> none  [the longest x1 0.83 us: local(): lng = lax.dynamic_slice_in_dim(lengths, first, ROWS_DEV, 0)]
    another operation x3 -> x0, other arithmetic: 1.37 us -> none
where the time goes in v2:
time: 112 us; the launch traced here: 111 us
  Pallas kernels  108 us (96%)
  local copies, waits for them, and re-layouts  3.5 us (3%)
    pallas_call x1, Pallas kernels, local(): pl.pallas_call(kernel, out_shape=jax.ShapeDtypeStruct((TOKENS, 256), BF16...  108 us

profile of v2, /device:TPU:0, one launch (start us, length us, event | category | flops | bytes accessed | tf_op | source)
XLA Modules:
  0.0 111.1 jit_solution(1257591185298398967)
XLA Ops:
  0.0 1.8 %reshape.12.hid = bf16[512,256]{1,0:T(8,128)(2,1)} reshape(bf16[256,2,256]{2,1,0:T(2,128)(2,1)} %param.15) | data formatting | bytes 524288 | tf_op jit(solution)/shard_map/reshape | solution.py:674
  1.8 107.6 %shard_map.145 = bf16[512,256]{1,0:T(8,128)(2,1)} custom-call(bf16[512,256]{1,0:T(8,128)(2,1)} %reshape.12.hid, s32[1,256]{1,0:T(1,128)} %bitcast.15, s32[1,256]{1,0:T(1,128)} %bitcast.16, s32[4,1024]{1,0:T(4,128)} %bitcast.13, f32[264,128]{1,0:T(8,128)} %constant.4.clone.cos_tab, f32[264,128]{1,0:T(8,128)} %constant.5.clone.sin_tab, s32[1024]{0:T(1024)} %lengths.1, ...), custom_call_target="tpu_custom_call" | custom-call | tf_op jit(solution)/shard_map/pallas_call | solution.py:664
  109.3 1.8 %reshape.15 = bf16[256,2,256]{2,1,0:T(2,128)(2,1)} reshape(bf16[512,256]{1,0:T(8,128)(2,1)} %shard_map.145) | data formatting | bytes 524288 | tf_op jit(solution)/shard_map/reshape | solution.py:680

commit v3 on v2

v3 whole, which is shorter than its diff:
```python
import functools
import math

import jax
import jax.numpy as jnp
import numpy as np
from jax import lax
from jax.experimental import pallas as pl
from jax.experimental.pallas import tpu as pltpu
from jax.sharding import PartitionSpec as P

QUERY_HEADS = 64
KEY_VALUE_HEADS = 8
HEAD_SIZE = 128
RANK_LIMIT = 64
ADAPTERS = 32
STEPS = 2
RES = 4
ROWS_DEV = 8
TOKENS = 512
POOL = 32
ROPE_BASE = 500000.0
MESH = pl.DeviceIdType.MESH
F32 = jnp.float32
BF16 = jnp.bfloat16


def dot(a, b):
    return jnp.dot(a, b, preferred_element_type=F32)


def dot_nt(a, b):
    return lax.dot_general(a, b, (((1,), (1,)), ((), ())), preferred_element_type=F32)


def dot_tn(a, b):
    return lax.dot_general(a, b, (((0,), (0,)), ((), ())), preferred_element_type=F32)


def remote(src, dst, send, recv, device):
    return pltpu.make_async_remote_copy(
        src_ref=src, dst_ref=dst, send_sem=send, recv_sem=recv,
        device_id=device, device_id_type=MESH,
    )


def kernel(
    hid, adapters, buckets, table_v, cos_tab, sin_tab, lengths, table,
    qw, kt, vt, ow, down, upq, upv, pool,
    out,
    hb, wq, wqp, kvt, wo, pages, dn, uq, uv,
    cos_t, sin_t, lens, pids, back,
    acc, metap, lowsend, lowrecv, scown, screcv, lift, liftv,
    send1, recv1, qs, kvs, knf, vnf, att, send2, recv2, lhs,
    sb, rh, rf, ta, ta0, rah, raf, kvperm,
    loc, ags, agr, wxs, wxr, fws, fwr, lows, lowr, scs, scr, s1s, s1r, s2s, s2r, rss, rsr, plane_sem, all_sem,
):
    g = lax.axis_index("group")
    t = lax.axis_index("tensor")
    core = g % 2
    z = t // 16
    y = (t // 4) % 4
    x = t % 4
    zp = 1 - z
    tp = zp * 16 + y * 4 + x
    g2 = (g + 2) % 4
    gs = g + 1 - 2 * core

    def near(along_b, d):
        on_x = (1 - core) * (1 - along_b) + core * along_b
        on_y = 1 - on_x
        xx = (x + 4 + d * on_x) % 4
        yy = (y + 4 + d * on_y) % 4
        return (g, z * 16 + yy * 4 + xx)

    def slice_index(oa, ob):
        dx = oa * (1 - core) + ob * core
        dy = oa * core + ob * (1 - core)
        return ((y + dy) % 4) * 4 + (x + dx) % 4

    half = z * 4096
    local = [
        (qw.at[pl.ds(pl.multiple_of(half, 4096), 4096)], wq),
        (kt.at[:, pl.ds(pl.multiple_of(half, 4096), 4096)], kvt.at[pl.ds(pl.multiple_of(z * 64, 32), 32)]),
        (vt.at[:, pl.ds(pl.multiple_of(half, 4096), 4096)], kvt.at[pl.ds(pl.multiple_of(z * 64 + 32, 32), 32)]),
        (ow.at[:, pl.ds(pl.multiple_of(half, 4096), 4096)], wo.at[z]),
        (down, dn),
        (upq, uq),
        (upv, uv),
        (pool, pages),
    ]
    local = [pltpu.make_async_copy(s, d, loc.at[i]) for i, (s, d) in enumerate(local)]
    for i in (4, 0, 1, 2, 5, 6, 3, 7):
        local[i].start()

    barrier = pltpu.get_barrier_semaphore()

    def ring_x(d):
        return (g, z * 16 + y * 4 + (x + d) % 4)

    def ring_y(d):
        return (g, z * 16 + ((y + d) % 4) * 4 + x)

    def line_z(d):
        zz = (2 * (g // 2) + z + d // 2) % 4
        return ((zz // 2) * 2 + (core + d) % 2, (zz % 2) * 16 + y * 4 + x)

    def greet(sem, device):
        pl.semaphore_signal(sem, inc=1, device_id=device, device_id_type=MESH)

    for d in range(1, 4):
        greet(barrier, ring_x(d))
        greet(barrier, ring_y(d))
    for d in range(1, 8):
        greet(barrier, line_z(d))

    def iota(shape, dim):
        return lax.broadcasted_iota(jnp.int32, shape, dim)

    tok = iota((8, TOKENS), 1)
    spread = (iota((256, TOKENS), 0) == iota((256, TOKENS), 1) // 2).astype(BF16)
    ahead = (
        (iota((256, TOKENS), 0) // 8 == iota((256, TOKENS), 1) // 16)
        & (iota((256, TOKENS), 0) < iota((256, TOKENS), 1) // 2)
    ).astype(BF16)
    first_page = table_v[0:1, pl.ds(pl.multiple_of(g * 256, 256), 256)]
    moved = (first_page // POOL != g * 32 + iota((1, 256), 1) // 8).astype(F32)
    moved = jnp.broadcast_to(moved, (8, 256)).astype(BF16)
    resumed = dot(moved, spread).astype(jnp.int32)
    before = dot(moved, ahead).astype(jnp.int32)
    place = jnp.where(resumed == 1, before, (tok // 2) % 8 - before)
    pos = resumed * 256 + (tok // 16) * 8 + place * 2 + tok % 2
    perm = (iota((TOKENS, TOKENS), 0) == pos[0:1]).astype(BF16)
    mine = dot(perm, hid[...].reshape(TOKENS, 256)).astype(BF16)
    for h in range(2):
        hb[h, 0, 0] = mine[h * 256:(h + 1) * 256]

    def ag_copy(h, row, kind):
        along_b = 1 if row else 0
        oa = row - 1

        def at(o, rows=None):
            ref = hb.at[h, oa, o] if along_b else hb.at[h, o, 0]
            return ref if rows is None else ref.at[pl.ds(rows, 128)]

        if kind == 0:
            src, dst, d = at(0), at(1), -1
        elif kind == 1:
            src, dst, d = at(0), at(3), 1
        elif kind == 2:
            src, dst, d = at(1, 0), at(2, 0), -1
        else:
            src, dst, d = at(3, 128), at(2, 128), 1
        return remote(src, dst, ags.at[h, row, kind], agr.at[h, row, kind], near(along_b, d))

    ag = [[[ag_copy(h, row, kind) for kind in range(4)] for row in range(5)] for h in range(2)]

    def arrive(h, row, kind):
        ag[h][row][kind].wait_recv()

    def own(h):
        for row in (0, 1):
            for kind in (0, 1):
                ag[h][row][kind].start()

    def first_ring(h):
        arrive(h, 0, 0)
        ag[h][0][2].start()
        ag[h][2][0].start()
        ag[h][2][1].start()
        arrive(h, 0, 1)
        ag[h][0][3].start()
        ag[h][4][0].start()
        ag[h][4][1].start()
        forward(h, 0)

    def forward(h, oa):
        for kind in (0, 1):
            arrive(h, 1 + oa, kind)
            ag[h][1 + oa][kind + 2].start()

    def first_ring_far(h):
        arrive(h, 0, 2)
        arrive(h, 0, 3)
        ag[h][3][0].start()
        ag[h][3][1].start()

    def along(row):
        wide = jnp.broadcast_to(row.astype(F32), (128, 256)).astype(BF16)
        return dot_nt(perm, dot(wide, spread).astype(BF16))

    metap[:, :128] = along(adapters[...])
    lane = iota((TOKENS, 128), 1)
    idxi = metap[:, :128].astype(jnp.int32)

    local[4].wait()

    def low_part(first, count):
        total = None
        for a in range(first, first + count, 2):
            maps = jnp.concatenate([dn[a], dn[a + 1]], axis=1)
            part = jnp.concatenate([dot(hb[h, 0, 0], maps) for h in range(2)], axis=0)
            part = jnp.where(idxi == a, part[:, :128], 0.0) + jnp.where(idxi == a + 1, part[:, 128:], 0.0)
            total = part if total is None else total + part
        return total

    low = low_part(0, ADAPTERS)
    for l in range(2):
        lowsend[:, l] = low[l * 256:(l + 1) * 256].reshape(32, 8, 128).astype(BF16)
    metap[:, 128:] = along(buckets[...])

    pl.semaphore_wait(barrier, 13)
    own(0)
    for d in range(1, 4):
        greet(plane_sem, ring_y(d))

    def wx_pieces(zq, q, zd):
        c0 = pl.multiple_of(zd * 4096 + q * 1024, 1024)
        d0 = pl.multiple_of(q * 1024, 1024)
        r0 = pl.multiple_of(q * 64, 64)
        return [
            (qw.at[pl.ds(c0, 1024)], wqp.at[pl.ds(d0, 1024)]),
            (kt.at[:, pl.ds(c0, 1024)], kvt.at[pl.ds(pl.multiple_of(zq * 64, 32), 32), pl.ds(d0, 1024)]),
            (vt.at[:, pl.ds(c0, 1024)], kvt.at[pl.ds(pl.multiple_of(zq * 64 + 32, 32), 32), pl.ds(d0, 1024)]),
            (ow.at[pl.ds(r0, 64), pl.ds(pl.multiple_of(zd * 4096, 4096), 4096)], wo.at[zq, pl.ds(r0, 64)]),
        ]

    def wx_copies(i):
        s, d = wx_pieces(z, g, zp)[i]
        return [remote(s, d, wxs.at[i, j], wxr.at[i, j], (gd, tp)) for j, gd in enumerate((g, g2))]

    def wx_arrivals(i):
        res = []
        for j, q in enumerate((g, g2)):
            s, d = wx_pieces(zp, q, z)[i]
            res.append(remote(s, d, wxs.at[i, j], wxr.at[i, j], (g, tp)))
        return res

    def fw_copies(i):
        res = []
        for j, q in enumerate((g, g2)):
            _, d = wx_pieces(zp, q, z)[i]
            res.append(remote(d, d, fws.at[i, j], fwr.at[i, j], (gs, t)))
        return res

    def fw_arrivals(i):
        res = []
        for j, q in enumerate((gs, (gs + 2) % 4)):
            _, d = wx_pieces(zp, q, z)[i]
            res.append(remote(d, d, fws.at[i, j], fwr.at[i, j], (gs, t)))
        return res

    for i in range(3):
        for c in wx_copies(i):
            c.start()
    own(1)

    def low_copy(o):
        d = (t + o) % 32
        return remote(lowsend.at[d], lowrecv.at[t], lows, lowr, (g, d))

    def low_start(o, carry):
        low_copy(o).start()
        return carry

    pl.semaphore_wait(plane_sem, 3)
    for d in range(1, 8):
        greet(all_sem, line_z(d))
    first_ring(0)
    pl.semaphore_wait(all_sem, 7)
    lax.fori_loop(1, 32, low_start, 0)
    lowrecv[t] = lowsend[t]
    first_ring(1)
    first_ring_far(0)
    forward(0, 1)
    forward(0, 3)

    remote(lowrecv.at[pl.ds(0, 31)], lowrecv.at[pl.ds(0, 31)], lows, lowr, (g, tp)).wait_recv()
    lane16 = lax.broadcasted_iota(jnp.int32, (8, 128), 1) % RANK_LIMIT
    for l in range(2):
        lowrank = jnp.sum(lowrecv[:, l].astype(F32), axis=0)
        bucket = metap[pl.ds(pl.multiple_of(l * 256 + t * 8, 8), 8), 128:]
        scaled = jnp.where(lane16.astype(F32) < bucket, lowrank * (0.5 * RANK_LIMIT) / bucket, 0.0)
        scown[l] = scaled.astype(BF16)

    def sc_copy(o):
        d = (t + o) % 32
        return remote(scown, screcv.at[t], scs, scr, (g, d))

    def sc_start(o, carry):
        sc_copy(o).start()
        return carry

    lax.fori_loop(1, 32, sc_start, 0)
    screcv[t] = scown[...]

    first_ring_far(1)
    forward(0, 2)
    forward(1, 1)
    forward(1, 3)
    base = (g * 32 + t) * POOL
    for l in range(2):
        gg = (g + 4 - l) % 4
        first = gg * 256 + t * ROWS_DEV
        marks, spots = [], []
        count = jnp.int32(0)
        for k in range(ROWS_DEV):
            mark = jnp.where(table[0, first + k] // POOL != gg * 32 + t, 1, 0)
            marks.append(mark)
            spots.append(jnp.where(mark == 1, count, k - count))
            count = count + mark
        for i in range(RES):
            mine = [(marks[k] == l) & (spots[k] == i) for k in range(ROWS_DEV)]
            row = l * RES + i
            lens[row] = sum(jnp.where(mine[k], lengths[first + k], 0) for k in range(ROWS_DEV))
            for j in range(4):
                page = sum(jnp.where(mine[k], table[j, first + k], 0) for k in range(ROWS_DEV))
                pids[row, j] = jnp.clip(page - base, 0, POOL - 1)
            cos_t[2 * row:2 * row + 2, :] = cos_tab[pl.ds(lens[row], 2), :]
            sin_t[2 * row:2 * row + 2, :] = sin_tab[pl.ds(lens[row], 2), :]

    eye = (iota((TOKENS, TOKENS), 0) == iota((TOKENS, TOKENS), 1)).astype(BF16)
    back[...] = dot_nt(eye, perm).astype(BF16)
    i0 = iota((512, 512), 0)
    target = ((i0 // 32) % 2) * 256 + ((i0 // 64) % 2) * 128 + (i0 // 128) * 32 + i0 % 32
    kvperm[...] = (target == iota((512, 512), 1)).astype(BF16)

    for i in (0, 1, 2):
        local[i].wait()
        for a, c in zip(wx_arrivals(i), fw_copies(i)):
            a.wait_recv()
            c.start()
    for c in wx_copies(3):
        c.start()
    forward(1, 2)

    remote(screcv.at[pl.ds(0, 31)], screcv.at[pl.ds(0, 31)], scs, scr, (g, tp)).wait_recv()
    local[5].wait()
    local[6].wait()
    sc = jnp.concatenate([screcv[:, l].astype(F32).reshape(256, 128) for l in range(2)], axis=0)
    swapped = pltpu.roll(sc, 64, 1)
    sq = jnp.where(lane < 64, sc, swapped)
    svk = jnp.where(lane < 64, swapped, 0.0).astype(BF16)[:, :64]
    lift[...] = jnp.zeros(lift.shape, F32)

    def lift_step(j, carry):
        two = [jnp.where(idxi == 4 * j + 2 * e + lane // 64, sq, 0.0).astype(BF16) for e in range(2)]
        lift[...] = lift[...] + dot(jnp.concatenate(two, axis=1), uq[pl.ds(pl.multiple_of(j * 256, 256), 256)])
        return carry

    lax.fori_loop(0, ADAPTERS // 4, lift_step, 0, unroll=2)
    liftv[...] = jnp.zeros(liftv.shape, F32)
    def liftv_step(j, carry):
        part = dot_nt(svk, uv[pl.ds(pl.multiple_of(j * 128, 128), 128)])
        liftv[...] = liftv[...] + jnp.where(idxi == 4 * j + lane // 32, part, 0.0)
        return carry

    lax.fori_loop(0, ADAPTERS // 4, liftv_step, 0, unroll=2)
    lv = liftv[...]
    lv = lv + pltpu.roll(lv, 64, 1)
    lv = lv + pltpu.roll(lv, 32, 1)
    place = lane // 32 == 2 * z + 1
    liftv[...] = jnp.where(place, lv, 0.0)
    for i in (0, 1, 2):
        for a in fw_arrivals(i):
            a.wait_recv()
    acc[...] = jnp.zeros(acc.shape, F32)

    def project(h, oa, ob):
        k0 = pl.multiple_of(slice_index(oa, ob) * 256, 256)
        x_in = hb[h, oa, ob]
        rows = slice(h * 256, (h + 1) * 256)
        acc[rows, 0:256] = acc[rows, 0:256] + dot(x_in, wq[pl.ds(k0, 256)])
        acc[rows, 256:512] = acc[rows, 256:512] + dot(x_in, wqp[pl.ds(k0, 256)])
        acc[rows, 512:640] = acc[rows, 512:640] + dot_nt(x_in, kvt[:, pl.ds(k0, 256)])


    def message(l, v, block):
        send1[l, :, block] = v.reshape(32, 8, 128).astype(BF16)

    def s1_copy(l, o):
        d = (t + o) % 32
        return remote(send1.at[l, d], recv1.at[l, t], s1s.at[l], s1r.at[l], ((g + l) % 4, d))

    def project_near(h):
        for oa in range(4):
            project(h, oa, 0)
        for oa in (0, 1, 3, 2):
            project(h, oa, 1)
            project(h, oa, 3)

    def project_far(h):
        for oa in (0, 1, 3, 2):
            arrive(h, 1 + oa, 2)
            arrive(h, 1 + oa, 3)
            project(h, oa, 2)

    def scatter_rows(l):
        rows = slice(l * 256, (l + 1) * 256)
        for j in range(2):
            message(l, acc[rows, j * 128:(j + 1) * 128] + lift[rows, j * 128:(j + 1) * 128], 2 * z + j)
            message(l, acc[rows, 256 + j * 128:256 + (j + 1) * 128], 2 * zp + j)
        message(l, acc[rows, 512:640] + liftv[rows, :], 4)

        def start(o, carry):
            s1_copy(l, o).start()
            return carry

        lax.fori_loop(1, 32, start, 0)
        if l == 0:
            recv1[0, t] = send1[0, t]
        else:
            s1_copy(1, 0).start()

    def rows_arrive(recv, send_sem, recv_sem, l):
        ref = recv.at[0, pl.ds(0, 31)] if l == 0 else recv.at[1]
        return remote(ref, ref, send_sem.at[l], recv_sem.at[l], (g, tp))

    head_of = iota((128, 128), 0) % 64
    cache_pos = iota((272, 128), 0)
    step = iota((272, 128), 1) // 64

    def attend(l):
        cos8 = cos_t[l * 8:(l + 1) * 8, :]
        sin8 = sin_t[l * 8:(l + 1) * 8, :]
        for yx in range(16):
            m = recv1[l, yx].astype(F32) + recv1[l, 16 + yx].astype(F32)
            m = m.astype(BF16).astype(F32)
            q = m[:4]
            q = q * cos8[None] + pltpu.roll(q, 64, 2) * sin8[None]
            for zj in range(4):
                head = (zj // 2) * 32 + yx * 2 + zj % 2
                r0 = l * 512 + head * 8
                qs[r0:r0 + 8, :] = q[zj].astype(BF16).astype(F32)
            yy, xx = yx // 4, yx % 4
            r0 = (l * 4 + yy) * 8
            kvs[r0:r0 + 8, xx * 128:(xx + 1) * 128] = m[4]
        kvp = dot(kvs[l * 32:(l + 1) * 32, :].astype(BF16), kvperm[...])
        for yy in range(4):
            r0 = yy * 8
            for zz in range(2):
                k = kvp[r0:r0 + 8, zz * 128:(zz + 1) * 128]
                k = k * cos8 + pltpu.roll(k, 64, 1) * sin8
                n = zz * 4 + yy
                knf[l, 0:8, n * 128:(n + 1) * 128] = k
                vnf[l, 0:8, n * 128:(n + 1) * 128] = kvp[r0:r0 + 8, 256 + zz * 128:256 + (zz + 1) * 128]
        knf[l, 8:16, :] = jnp.zeros((8, 1024), F32)
        vnf[l, 8:16, :] = jnp.zeros((8, 1024), F32)
        knew = knf[l].astype(BF16)
        vnew = vnf[l].astype(BF16)

        for ii in range(RES):
            i = l * RES + ii
            q = jnp.concatenate(
                [qs[pl.ds(l * 512 + 2 * ii + st, 64, stride=8), :] for st in range(2)], axis=0
            )
            bd = jnp.concatenate(
                [jnp.where(head_of // 8 == n, q, 0.0).astype(BF16) for n in range(8)], axis=1
            )
            keys = jnp.concatenate([pages[pids[i, j], :, :1024] for j in range(4)] + [knew], axis=0)
            values = jnp.concatenate([pages[pids[i, j], :, 1024:] for j in range(4)] + [vnew], axis=0)
            scores = dot_nt(keys, bd) * HEAD_SIZE ** (-0.5)
            first = 256 + 2 * ii
            usable = (
                (cache_pos < lens[i])
                | (cache_pos == first)
                | ((cache_pos == first + 1) & (step == 1))
            )
            top = jnp.max(jnp.where(usable, scores, -jnp.inf), axis=0, keepdims=True)
            e = jnp.where(usable, jnp.exp(scores - top), 0.0)
            probs = (e / jnp.sum(e, axis=0, keepdims=True)).astype(BF16)
            o = dot_tn(probs, values)
            for st in range(2):
                for n in range(8):
                    r0 = (2 * i + st) * 64 + n * 8
                    att[r0:r0 + 8, :] = o[st * 64 + n * 8:st * 64 + (n + 1) * 8, n * 128:(n + 1) * 128]

        def pack(yx, carry):
            for zj in range(4):
                head = (zj // 2) * 32 + yx * 2 + zj % 2
                send2[l, yx, zj] = att[pl.ds(l * 512 + head, 8, stride=64), :].astype(BF16)
            return carry

        lax.fori_loop(0, 16, pack, 0, unroll=4)

    def s2_copy(l, o):
        d = (t + o) % 32
        return remote(send2.at[l, d % 16], recv2.at[l, t], s2s.at[l], s2r.at[l], ((g + 4 - l) % 4, d))

    def scatter_heads(l):
        def start(o, carry):
            s2_copy(l, o).start()
            return carry

        lax.fori_loop(1, 32, start, 0)
        if l == 0:
            recv2[0, t] = send2[0, t % 16]
        else:
            s2_copy(1, 0).start()

    def build(l):
        rows_arrive(recv2, s2s, s2r, l).wait_recv()

        def some(k, carry):
            r0 = pl.multiple_of(l * 256 + k * 16, 16)
            for zj in range(4):
                both = jnp.concatenate([recv2[l, 2 * k + e, zj].astype(F32) for e in range(2)], axis=0)
                lhs[pl.ds(r0, 16), zj * 128:(zj + 1) * 128] = both.astype(BF16)
            return carry

        lax.fori_loop(0, 16, some, 0, unroll=4)

    def partial(h, oa, ob):
        c0 = pl.multiple_of(slice_index(oa, ob) * 256, 256)
        rows = slice(h * 256, (h + 1) * 256)
        return dot(lhs[rows, :256], wo[0, :, pl.ds(c0, 256)]) + dot(lhs[rows, 256:], wo[1, :, pl.ds(c0, 256)])

    def rs_copy(h, row, kind):
        along_b = 1 if row else 0
        oa = row - 1

        def src(o, rows=None):
            ref = sb.at[h, oa, o] if along_b else ta.at[h, o]
            return ref if rows is None else ref.at[pl.ds(rows, 128)]

        halves = rh.at[h, oa] if along_b else rah.at[h]
        fulls = rf.at[h, oa] if along_b else raf.at[h]
        if kind == 0:
            s, d, way = src(2, 0), halves.at[0], -1
        elif kind == 1:
            s, d, way = src(2, 128), halves.at[1], 1
        elif kind == 2:
            s, d, way = src(3), fulls.at[0], -1
        else:
            s, d, way = src(1), fulls.at[1], 1
        return remote(s, d, rss.at[h, row, kind], rsr.at[h, row, kind], near(along_b, way))

    rs = [[[rs_copy(h, row, kind) for kind in range(4)] for row in range(5)] for h in range(2)]
    order = (2, 1, 3, 0)

    def reduce_far(h):
        for oa in order:
            sb[h, oa, 2] = partial(h, oa, 2).astype(BF16)
            rs[h][1 + oa][0].start()
            rs[h][1 + oa][1].start()

    def reduce_near(h):
        for oa in order:
            part = partial(h, oa, 3)
            rs[h][1 + oa][0].wait_recv()
            sb[h, oa, 3, 0:128] = (part[0:128] + rh[h, oa, 0].astype(F32)).astype(BF16)
            sb[h, oa, 3, 128:256] = part[128:256].astype(BF16)
            rs[h][1 + oa][2].start()
            part = partial(h, oa, 1)
            rs[h][1 + oa][1].wait_recv()
            sb[h, oa, 1, 0:128] = part[0:128].astype(BF16)
            sb[h, oa, 1, 128:256] = (part[128:256] + rh[h, oa, 1].astype(F32)).astype(BF16)
            rs[h][1 + oa][3].start()

    def total(h, oa):
        part = partial(h, oa, 0)
        rs[h][1 + oa][2].wait_recv()
        rs[h][1 + oa][3].wait_recv()
        return part + rf[h, oa, 0].astype(F32) + rf[h, oa, 1].astype(F32)

    def reduce_first(h):
        ta[h, 2] = total(h, 2).astype(BF16)
        rs[h][0][0].start()
        rs[h][0][1].start()

    def reduce_last(h):
        part = total(h, 1)
        rs[h][0][1].wait_recv()
        ta[h, 1, 0:128] = part[0:128].astype(BF16)
        ta[h, 1, 128:256] = (part[128:256] + rah[h, 1].astype(F32)).astype(BF16)
        rs[h][0][3].start()
        part = total(h, 3)
        rs[h][0][0].wait_recv()
        ta[h, 3, 0:128] = (part[0:128] + rah[h, 0].astype(F32)).astype(BF16)
        ta[h, 3, 128:256] = part[128:256].astype(BF16)
        rs[h][0][2].start()
        ta0[h] = total(h, 0)

    def result(h):
        rs[h][0][2].wait_recv()
        rs[h][0][3].wait_recv()
        return (ta0[h] + raf[h, 0].astype(F32) + raf[h, 1].astype(F32)).astype(BF16)

    project_near(0)
    project_far(0)
    scatter_rows(0)
    project_near(1)
    project_far(1)
    scatter_rows(1)
    local[7].wait()
    rows_arrive(recv1, s1s, s1r, 0).wait_recv()
    attend(0)
    scatter_heads(0)
    rows_arrive(recv1, s1s, s1r, 1).wait_recv()
    attend(1)
    scatter_heads(1)
    local[3].wait()
    for a, c in zip(wx_arrivals(3), fw_copies(3)):
        a.wait_recv()
        c.start()
    for a in fw_arrivals(3):
        a.wait_recv()
    build(0)
    reduce_far(0)
    reduce_near(0)
    build(1)
    reduce_far(1)
    reduce_first(0)
    reduce_last(0)
    reduce_near(1)
    reduce_first(1)
    reduce_last(1)
    low_half = result(0)
    final = jnp.concatenate([low_half, result(1)], axis=0)
    out[...] = dot(back[...], final).astype(BF16).reshape(256, STEPS, 256)

    for h in range(2):
        for row in range(5):
            for kind in range(4):
                ag[h][row][kind].wait_send()
                rs[h][row][kind].wait_send()
    for i in range(4):
        for c in wx_copies(i) + fw_copies(i):
            c.wait_send()
    remote(lowrecv.at[pl.ds(0, 31)], lowrecv.at[pl.ds(0, 31)], lows, lowr, (g, tp)).wait_send()
    remote(screcv.at[pl.ds(0, 31)], screcv.at[pl.ds(0, 31)], scs, scr, (g, tp)).wait_send()
    for l in range(2):
        rows_arrive(recv1, s1s, s1r, l).wait_send()
        rows_arrive(recv2, s2s, s2r, l).wait_send()


def scratch():
    v = pltpu.VMEM
    dma = pltpu.SemaphoreType.DMA
    return [
        v((2, 4, 4, 256, 256), BF16),
        v((4096, 256), BF16),
        v((4096, 256), BF16),
        v((128, 4096), BF16),
        v((2, 256, 4096), BF16),
        v((32, 64, 2048), BF16),
        v((32, 256, 128), BF16),
        v((2048, 256), BF16),
        v((1024, 64), BF16),
        v((16, 128), F32),
        v((16, 128), F32),
        pltpu.SMEM((8,), jnp.int32),
        pltpu.SMEM((8, 4), jnp.int32),
        v((512, 512), BF16),
        v((512, 640), F32),
        v((512, 256), F32),
        v((32, 2, 8, 128), BF16),
        v((32, 2, 8, 128), BF16),
        v((2, 8, 128), BF16),
        v((32, 2, 8, 128), BF16),
        v((512, 256), F32),
        v((512, 128), F32),
        v((2, 32, 5, 8, 128), BF16),
        v((2, 32, 5, 8, 128), BF16),
        v((1024, 128), F32),
        v((64, 512), F32),
        v((2, 16, 1024), F32),
        v((2, 16, 1024), F32),
        v((1024, 128), F32),
        v((2, 16, 4, 8, 128), BF16),
        v((2, 32, 4, 8, 128), BF16),
        v((512, 512), BF16),
        v((2, 4, 4, 256, 256), BF16),
        v((2, 4, 2, 128, 256), BF16),
        v((2, 4, 2, 256, 256), BF16),
        v((2, 4, 256, 256), BF16),
        v((2, 256, 256), F32),
        v((2, 2, 128, 256), BF16),
        v((2, 2, 256, 256), BF16),
        v((512, 512), BF16),
        dma((8,)),
        dma((2, 5, 4)), dma((2, 5, 4)),
        dma((4, 2)), dma((4, 2)),
        dma((4, 2)), dma((4, 2)),
        dma, dma, dma, dma,
        dma((2,)), dma((2,)),
        dma((2,)), dma((2,)),
        dma((2, 5, 4)), dma((2, 5, 4)),
        pltpu.SemaphoreType.REGULAR,
        pltpu.SemaphoreType.REGULAR,
    ]


def local(
    hidden, query_weight, key_weight, value_weight, output_weight, adapter_down_maps,
    adapter_up_query, adapter_up_value, key_value_pages, row_adapter_index,
    row_rank_bucket, lengths, row_page_index,
):
    positions = np.arange(264, dtype=np.float32)
    inverse_freq = np.exp(np.float32(-math.log(ROPE_BASE)) * np.arange(64, dtype=np.float32) / np.float32(64))
    angles = positions[:, None] * np.concatenate([inverse_freq, inverse_freq])[None].astype(np.float32)
    sign = np.where(np.arange(128) < 64, -1.0, 1.0)[None]
    cos_tab = jnp.asarray(np.cos(angles), F32)
    sin_tab = jnp.asarray(np.sin(angles) * sign, F32)

    vm = pl.BlockSpec(memory_space=pltpu.VMEM)
    sm = pl.BlockSpec(memory_space=pltpu.SMEM)
    hbm = pl.BlockSpec(memory_space=pl.ANY)
    res = pl.pallas_call(
        kernel,
        out_shape=jax.ShapeDtypeStruct((256, STEPS, 256), BF16),
        in_specs=[vm] * 6 + [sm] * 2 + [hbm] * 8,
        out_specs=vm,
        scratch_shapes=scratch(),
        compiler_params=pltpu.CompilerParams(
            collective_id=0, has_side_effects=True, vmem_limit_bytes=60 * 1024 * 1024
        ),
    )(
        hidden, row_adapter_index[None, :], row_rank_bucket[None, :], row_page_index.T,
        cos_tab, sin_tab, lengths, row_page_index.T,
        query_weight, key_weight.T, value_weight.T, output_weight, adapter_down_maps,
        adapter_up_query.reshape(2048, 256),
        adapter_up_value.transpose(0, 2, 1).reshape(1024, 64), key_value_pages,
    )
    return res


def solution(mesh):
    in_specs = (
        P("group", None, "tensor"),
        P(None, "tensor"),
        P(None, "tensor"),
        P(None, "tensor"),
        P("tensor", None),
        P(None, "tensor", None),
        P(None, None, "tensor"),
        P(None, None, "tensor"),
        P(("group", "tensor"), None, None),
        P("group"),
        P("group"),
        P(),
        P(),
    )
    out_specs = P("group", None, "tensor")
    return jax.shard_map(local, mesh=mesh, in_specs=in_specs, out_specs=out_specs, check_vma=False)
```

time: 112 us -> 91.3 us (0.82)
  Pallas kernels: 108 us -> 89.3 us
  local copies, waits for them, and re-layouts: 3.5 us -> 1.83 us
    pallas_call x1, Pallas kernels: 108 us -> 89.3 us  [local(): pl.pallas_call(kernel, out_shape=jax.ShapeDtypeStruct((256, STEPS, 256),...]
    reshape x2 -> x0, local copies, waits for them, and re-layouts: 3.5 us -> none  [the longest x1 1.75 us: local(): return res.reshape(256, STEPS, 256)]
    unnamed x0 -> x1, local copies, waits for them, and re-layouts: none -> 1.83 us
where the time goes in v3:
time: 91.3 us; the launch traced here: 91.1 us
  Pallas kernels  89.3 us (98%)
  local copies, waits for them, and re-layouts  1.83 us (2%)
    pallas_call x1, Pallas kernels, local(): pl.pallas_call(kernel, out_shape=jax.ShapeDtypeStruct((256, STEPS, 256),...  89.3 us
    unnamed x1, local copies, waits for them, and re-layouts  1.83 us

profile of v3, /device:TPU:0, one launch (start us, length us, event | category | flops | bytes accessed | tf_op | source)
XLA Modules:
  0.0 91.1 jit_solution(17282144795235953744)
XLA Ops:
  0.0 89.3 %shard_map.145 = bf16[256,2,256]{2,1,0:T(2,128)(2,1)} custom-call(bf16[256,2,256]{2,1,0:T(2,128)(2,1)} %hid.1, s32[1,256]{1,0:T(1,128)} %bitcast.15, s32[1,256]{1,0:T(1,128)} %bitcast.16, s32[4,1024]{1,0:T(4,128)} %bitcast.13, f32[264,128]{1,0:T(8,128)} %constant.4.clone.cos_tab, f32[264,128]{1,0:T(8,128)} %constant.5.clone.sin_tab, s32[1024]{0:T(1024)} %lengths.1, ...), custom_call_target="tpu_custom_call" | custom-call | tf_op jit(solution)/shard_map/pallas_call | solution.py:709
  89.3 1.8 %copy.17 = bf16[256,2,256]{2,1,0:T(2,128)(2,1)} copy(bf16[256,2,256]{2,1,0:T(2,128)(2,1)} %shard_map.145) | data formatting | bytes 524288

commit v4 on v3

--- a/solution.py
+++ b/solution.py
@@ -129,7 +129,7 @@
     resumed = dot(moved, spread).astype(jnp.int32)
     before = dot(moved, ahead).astype(jnp.int32)
     place = jnp.where(resumed == 1, before, (tok // 2) % 8 - before)
-    pos = resumed * 256 + (tok // 16) * 8 + place * 2 + tok % 2
+    pos = (1 - resumed) * 256 + (tok // 16) * 8 + place * 2 + tok % 2
     perm = (iota((TOKENS, TOKENS), 0) == pos[0:1]).astype(BF16)
     mine = dot(perm, hid[...].reshape(TOKENS, 256)).astype(BF16)
     for h in range(2):
@@ -268,7 +268,7 @@
         greet(all_sem, line_z(d))
     first_ring(0)
     pl.semaphore_wait(all_sem, 7)
-    lax.fori_loop(1, 32, low_start, 0)
+    lax.fori_loop(1, 32, low_start, 0, unroll=8)
     lowrecv[t] = lowsend[t]
     first_ring(1)
     first_ring_far(0)
@@ -291,8 +291,10 @@
         sc_copy(o).start()
         return carry
 
-    lax.fori_loop(1, 32, sc_start, 0)
+    lax.fori_loop(1, 32, sc_start, 0, unroll=8)
     screcv[t] = scown[...]
+    for c in wx_copies(3):
+        c.start()
 
     first_ring_far(1)
     forward(0, 2)
@@ -300,7 +302,7 @@
     forward(1, 3)
     base = (g * 32 + t) * POOL
     for l in range(2):
-        gg = (g + 4 - l) % 4
+        gg = (g + 3 + l) % 4
         first = gg * 256 + t * ROWS_DEV
         marks, spots = [], []
         count = jnp.int32(0)
@@ -310,7 +312,7 @@
             spots.append(jnp.where(mark == 1, count, k - count))
             count = count + mark
         for i in range(RES):
-            mine = [(marks[k] == l) & (spots[k] == i) for k in range(ROWS_DEV)]
+            mine = [(marks[k] == 1 - l) & (spots[k] == i) for k in range(ROWS_DEV)]
             row = l * RES + i
             lens[row] = sum(jnp.where(mine[k], lengths[first + k], 0) for k in range(ROWS_DEV))
             for j in range(4):
@@ -330,8 +332,6 @@
         for a, c in zip(wx_arrivals(i), fw_copies(i)):
             a.wait_recv()
             c.start()
-    for c in wx_copies(3):
-        c.start()
     forward(1, 2)
 
     remote(screcv.at[pl.ds(0, 31)], screcv.at[pl.ds(0, 31)], scs, scr, (g, tp)).wait_recv()
@@ -380,7 +380,7 @@
 
     def s1_copy(l, o):
         d = (t + o) % 32
-        return remote(send1.at[l, d], recv1.at[l, t], s1s.at[l], s1r.at[l], ((g + l) % 4, d))
+        return remote(send1.at[l, d], recv1.at[l, t], s1s.at[l], s1r.at[l], ((g + 1 - l) % 4, d))
 
     def project_near(h):
         for oa in range(4):
@@ -406,14 +406,14 @@
             s1_copy(l, o).start()
             return carry
 
-        lax.fori_loop(1, 32, start, 0)
-        if l == 0:
-            recv1[0, t] = send1[0, t]
+        lax.fori_loop(1, 32, start, 0, unroll=8)
+        if l == 1:
+            recv1[1, t] = send1[1, t]
         else:
-            s1_copy(1, 0).start()
+            s1_copy(0, 0).start()
 
     def rows_arrive(recv, send_sem, recv_sem, l):
-        ref = recv.at[0, pl.ds(0, 31)] if l == 0 else recv.at[1]
+        ref = recv.at[1, pl.ds(0, 31)] if l == 1 else recv.at[0]
         return remote(ref, ref, send_sem.at[l], recv_sem.at[l], (g, tp))
 
     head_of = iota((128, 128), 0) % 64
@@ -458,7 +458,7 @@
                 [jnp.where(head_of // 8 == n, q, 0.0).astype(BF16) for n in range(8)], axis=1
             )
             keys = jnp.concatenate([pages[pids[i, j], :, :1024] for j in range(4)] + [knew], axis=0)
-            values = jnp.concatenate([pages[pids[i, j], :, 1024:] for j in range(4)] + [vnew], axis=0)
+            values = jnp.concatenate([pages[pids[i, j], :, 1024:] for j in range(4)], axis=0)
             scores = dot_nt(keys, bd) * HEAD_SIZE ** (-0.5)
             first = 256 + 2 * ii
             usable = (
@@ -469,7 +469,7 @@
             top = jnp.max(jnp.where(usable, scores, -jnp.inf), axis=0, keepdims=True)
             e = jnp.where(usable, jnp.exp(scores - top), 0.0)
             probs = (e / jnp.sum(e, axis=0, keepdims=True)).astype(BF16)
-            o = dot_tn(probs, values)
+            o = dot_tn(probs[:256], values) + dot_tn(probs[256:], vnew)
             for st in range(2):
                 for n in range(8):
                     r0 = (2 * i + st) * 64 + n * 8
@@ -485,18 +485,18 @@
 
     def s2_copy(l, o):
         d = (t + o) % 32
-        return remote(send2.at[l, d % 16], recv2.at[l, t], s2s.at[l], s2r.at[l], ((g + 4 - l) % 4, d))
+        return remote(send2.at[l, d % 16], recv2.at[l, t], s2s.at[l], s2r.at[l], ((g + 3 + l) % 4, d))
 
     def scatter_heads(l):
         def start(o, carry):
             s2_copy(l, o).start()
             return carry
 
-        lax.fori_loop(1, 32, start, 0)
-        if l == 0:
-            recv2[0, t] = send2[0, t % 16]
+        lax.fori_loop(1, 32, start, 0, unroll=8)
+        if l == 1:
+            recv2[1, t] = send2[1, t % 16]
         else:
-            s2_copy(1, 0).start()
+            s2_copy(0, 0).start()
 
     def build(l):
         rows_arrive(recv2, s2s, s2r, l).wait_recv()
@@ -596,13 +596,13 @@
     rows_arrive(recv1, s1s, s1r, 0).wait_recv()
     attend(0)
     scatter_heads(0)
-    rows_arrive(recv1, s1s, s1r, 1).wait_recv()
-    attend(1)
-    scatter_heads(1)
     local[3].wait()
     for a, c in zip(wx_arrivals(3), fw_copies(3)):
         a.wait_recv()
         c.start()
+    rows_arrive(recv1, s1s, s1r, 1).wait_recv()
+    attend(1)
+    scatter_heads(1)
     for a in fw_arrivals(3):
         a.wait_recv()
     build(0)
@@ -611,8 +611,8 @@
     build(1)
     reduce_far(1)
     reduce_first(0)
+    reduce_near(1)
     reduce_last(0)
-    reduce_near(1)
     reduce_first(1)
     reduce_last(1)
     low_half = result(0)

time: 91.3 us -> 88.6 us (0.970)
  Pallas kernels: 89.3 us -> 86.4 us
    pallas_call x1, Pallas kernels: 89.3 us -> 86.4 us  [local(): pl.pallas_call(kernel, out_shape=jax.ShapeDtypeStruct((256, STEPS, 256),...]
where the time goes in v4:
time: 88.6 us; the launch traced here: 88.2 us
  Pallas kernels  86.4 us (98%)
  local copies, waits for them, and re-layouts  1.83 us (2%)
    pallas_call x1, Pallas kernels, local(): pl.pallas_call(kernel, out_shape=jax.ShapeDtypeStruct((256, STEPS, 256),...  86.4 us
    unnamed x1, local copies, waits for them, and re-layouts  1.83 us

profile of v4, /device:TPU:0, one launch (start us, length us, event | category | flops | bytes accessed | tf_op | source)
XLA Modules:
  0.0 88.2 jit_solution(11130025559673266692)
XLA Ops:
  0.0 86.4 %shard_map.145 = bf16[256,2,256]{2,1,0:T(2,128)(2,1)} custom-call(bf16[256,2,256]{2,1,0:T(2,128)(2,1)} %hid.1, s32[1,256]{1,0:T(1,128)} %bitcast.15, s32[1,256]{1,0:T(1,128)} %bitcast.16, s32[4,1024]{1,0:T(4,128)} %bitcast.13, f32[264,128]{1,0:T(8,128)} %constant.4.clone.cos_tab, f32[264,128]{1,0:T(8,128)} %constant.5.clone.sin_tab, s32[1024]{0:T(1024)} %lengths.1, ...), custom_call_target="tpu_custom_call" | custom-call | tf_op jit(solution)/shard_map/pallas_call | solution.py:709
  86.4 1.8 %copy.17 = bf16[256,2,256]{2,1,0:T(2,128)(2,1)} copy(bf16[256,2,256]{2,1,0:T(2,128)(2,1)} %shard_map.145) | data formatting | bytes 524288

commit v5 on v4

--- a/solution.py
+++ b/solution.py
@@ -327,12 +327,13 @@
     target = ((i0 // 32) % 2) * 256 + ((i0 // 64) % 2) * 128 + (i0 // 128) * 32 + i0 % 32
     kvperm[...] = (target == iota((512, 512), 1)).astype(BF16)
 
+    forward(1, 2)
+
     for i in (0, 1, 2):
         local[i].wait()
         for a, c in zip(wx_arrivals(i), fw_copies(i)):
             a.wait_recv()
             c.start()
-    forward(1, 2)
 
     remote(screcv.at[pl.ds(0, 31)], screcv.at[pl.ds(0, 31)], scs, scr, (g, tp)).wait_recv()
     local[5].wait()

time: 88.6 us -> 88.1 us (level)
  no operation moved by 1% of the time
where the time goes in v5:
time: 88.1 us; the launch traced here: 87.8 us
  Pallas kernels  85.9 us (98%)
  local copies, waits for them, and re-layouts  1.83 us (2%)
    pallas_call x1, Pallas kernels, local(): pl.pallas_call(kernel, out_shape=jax.ShapeDtypeStruct((256, STEPS, 256),...  85.9 us
    unnamed x1, local copies, waits for them, and re-layouts  1.83 us

profile of v5, /device:TPU:0, one launch (start us, length us, event | category | flops | bytes accessed | tf_op | source)
XLA Modules:
  0.0 87.8 jit_solution(9276135069381461612)
XLA Ops:
  0.0 85.9 %shard_map.145 = bf16[256,2,256]{2,1,0:T(2,128)(2,1)} custom-call(bf16[256,2,256]{2,1,0:T(2,128)(2,1)} %hid.1, s32[1,256]{1,0:T(1,128)} %bitcast.15, s32[1,256]{1,0:T(1,128)} %bitcast.16, s32[4,1024]{1,0:T(4,128)} %bitcast.13, f32[264,128]{1,0:T(8,128)} %constant.4.clone.cos_tab, f32[264,128]{1,0:T(8,128)} %constant.5.clone.sin_tab, s32[1024]{0:T(1024)} %lengths.1, ...), custom_call_target="tpu_custom_call" | custom-call | tf_op jit(solution)/shard_map/pallas_call | solution.py:710
  85.9 1.8 %copy.17 = bf16[256,2,256]{2,1,0:T(2,128)(2,1)} copy(bf16[256,2,256]{2,1,0:T(2,128)(2,1)} %shard_map.145) | data formatting | bytes 524288
